TPU v7x, 256 devices: a whole 4x4x8 slice. The times are simulated.
256 devices in a mesh: cols: 8 (over z_lo, core), space: 32 (over y, z_hi, x).
Axes of the slice: x: 4, y: 4, z: 8 (z_hi: 2, z_lo: 4; z = z_hi * 4 + z_lo), core: 2. Of those that a mesh axis runs over, the one named last changes fastest.
Arguments:
- mean_state: float32 [6, 512, 256], P(None, 'space', 'cols'), may hold values from -2 to 2
- covariance: float32 [128, 6, 512, 256], P('cols', None, 'space'), may hold values from -2 to 2
- land_mask: int32 [512, 256], replicated, may hold values 0 or 1
- stations: int32 [4096], P('space'), may hold values from 0 to 131071, as said below
- observed: float32 [4096], P('space'), may hold values from -5 to 5
- obs_weight: float32 [4096], P('space'), may hold values from 0.5 to 4
Outputs:
- mean_analysis: float32 [6, 512, 256], P(None, 'space', 'cols')
- covariance_analysis: float32 [128, 6, 512, 256], P('cols', None, 'space')
Inputs may be any that keep to these rules, and one draw needn't show every extreme that they name: Stations b * 128 to (b + 1) * 128 - 1 lie in grid rows b * 16 to (b + 1) * 16 - 1; several stations may share a cell.
All inputs are finite; a program needn't handle non-finite values.
Results may differ from a plain program's by a relative error of at most 0.0053.
Values may be sent and summed in bfloat16 or wider, within the bound.
A program may use at most 64 MiB of HBM per device.

v0:
```python
import jax
import jax.numpy as jnp
from jax import lax
from jax.sharding import PartitionSpec as P

ITERS = 4


time_step = 0.5
gravity = 1.0
reduced_gravity = 0.125
coriolis = 0.3
friction = 0.05
layer_depths = (1.0, 2.0)


def padded_2(block, sides, width):
    for axis, dim in sides:
        count = lax.axis_size(axis)
        forward = [(i, i + 1) for i in range(count - 1)]
        backward = [(target, source) for source, target in forward]
        low = lax.ppermute(
            lax.slice_in_dim(block, block.shape[dim] - width, None, axis=dim), axis, forward
        )
        high = lax.ppermute(lax.slice_in_dim(block, 0, width, axis=dim), axis, backward)
        block = jnp.concatenate([low, block, high], axis=dim)
    return block


def diff_rows(values):
    return 0.5 * (values[..., 2:, 1:-1] - values[..., :-2, 1:-1])


def diff_cols(values):
    return 0.5 * (values[..., 1:-1, 2:] - values[..., 1:-1, :-2])


def inner(values):
    return values[..., 1:-1, 1:-1]


def velocities(field, wet_cells):
    wet_inner = inner(wet_cells)
    surface = field[..., 0, :, :] + field[..., 3, :, :]
    pressure_top = gravity * surface
    pressure_pair = (pressure_top, pressure_top - reduced_gravity * field[..., 0, :, :])
    velocity_pairs = []
    for layer_index in range(2):
        zonal = inner(field[..., 3 * layer_index + 1, :, :])
        north = inner(field[..., 3 * layer_index + 2, :, :])
        pressure = pressure_pair[layer_index]
        zonal_new = wet_inner * (
            zonal + time_step * (-diff_rows(pressure) + coriolis * north - friction * zonal)
        )
        north_new = wet_inner * (
            north + time_step * (-diff_cols(pressure) - coriolis * zonal - friction * north)
        )
        velocity_pairs.append((zonal_new, north_new))
    return velocity_pairs


def mean_core(padded, wet_cells):
    velocity_pairs = velocities(padded, wet_cells)
    fields = []
    carried = []
    for layer_index in range(2):
        thickness = padded[3 * layer_index]
        column_depth = layer_depths[layer_index] + inner(thickness)
        zonal_new, north_new = velocity_pairs[layer_index]
        updated = thickness[2:-2, 2:-2] - time_step * (
            diff_rows(column_depth * zonal_new) + diff_cols(column_depth * north_new)
        )
        fields += [updated, zonal_new[1:-1, 1:-1], north_new[1:-1, 1:-1]]
        carried += [thickness[1:-1, 2:-2], zonal_new[:, 1:-1], north_new[:, 1:-1]]
    return (jnp.stack(fields), jnp.stack(carried))


def tangent_core(padded, carried, wet_cells):
    beside_all = jnp.pad(carried, ((0, 0), (0, 0), (1, 1)))
    velocity_pairs = velocities(padded, wet_cells)
    fields = []
    for layer_index in range(2):
        thickness = padded[..., 3 * layer_index, :, :]
        column_depth = layer_depths[layer_index] + beside_all[3 * layer_index]
        zonal_new, north_new = velocity_pairs[layer_index]
        flux_rows = column_depth * zonal_new + inner(thickness) * beside_all[3 * layer_index + 1]
        flux_cols = column_depth * north_new + inner(thickness) * beside_all[3 * layer_index + 2]
        updated = thickness[..., 2:-2, 2:-2] - time_step * (
            diff_rows(flux_rows) + diff_cols(flux_cols)
        )
        fields += [updated, zonal_new[..., 1:-1, 1:-1], north_new[..., 1:-1, 1:-1]]
    return jnp.stack(fields, axis=-3)


def advance_columns(columns, carried, wet_tile):
    padded = padded_2(columns, (("space", 2),), 2)
    padded = jnp.pad(padded, ((0, 0), (0, 0), (0, 0), (2, 2)))
    return tangent_core(padded, carried, wet_tile)


def local(mean_state, covariance, land_mask, stations, observed, obs_weight):
    local_cols = covariance.shape[0]
    tile_rows = covariance.shape[2]
    grid_cols = covariance.shape[3]
    piece_cols = mean_state.shape[2]
    total_cols = local_cols * lax.axis_size("cols")
    space_index = lax.axis_index("space")
    column_index = lax.axis_index("cols")
    land_float = land_mask.astype(jnp.float32)
    wet_all = jnp.pad(land_float, 2)
    first_row = space_index * tile_rows
    wet_tile = lax.dynamic_slice_in_dim(wet_all, first_row, tile_rows + 4, 0)
    columns = covariance
    wet_piece = lax.dynamic_slice(
        wet_all, (first_row, column_index * piece_cols), (tile_rows + 4, piece_cols + 4)
    )
    mean_now = mean_state
    for step_index in range(ITERS):
        padded = padded_2(mean_now, (("cols", 2), ("space", 1)), 2)
        mean_now, carried = mean_core(padded, wet_piece)
        carried = lax.all_gather(carried, "cols", axis=2, tiled=True)
        columns = advance_columns(columns, carried, wet_tile)
    surface = lax.all_gather(mean_now[0] + mean_now[3], "cols", axis=1, tiled=True)
    offset_stations = stations - first_row * grid_cols
    column_surface = (columns[:, 0] + columns[:, 3]).reshape(local_cols, tile_rows * grid_cols)
    sensed_local = jnp.take(column_surface, offset_stations, axis=1) * obs_weight[None, :]
    innovation = obs_weight * (observed - jnp.take(surface.reshape(-1), offset_stations))
    sensed = lax.all_gather(sensed_local, "cols", axis=0, tiled=True)
    products = jnp.dot(
        sensed, sensed.T, precision=lax.Precision.HIGHEST, preferred_element_type=jnp.float32
    )
    target_part = jnp.dot(
        sensed, innovation, precision=lax.Precision.HIGHEST, preferred_element_type=jnp.float32
    )
    gram_sum, target = lax.psum((products, target_part), "space")
    identity = jnp.eye(total_cols, dtype=jnp.float32)
    gram_matrix = identity + gram_sum
    lower_factor = lax.linalg.cholesky(gram_matrix)
    halfway = lax.linalg.triangular_solve(lower_factor, target[:, None], left_side=True, lower=True)
    weights = lax.linalg.triangular_solve(
        lower_factor, halfway, left_side=True, lower=True, transpose_a=True
    )[:, 0]
    inverse = lax.linalg.triangular_solve(lower_factor, identity, left_side=True, lower=True)
    transform_low = inverse.T.astype(jnp.bfloat16)
    weights_local = lax.dynamic_slice_in_dim(weights, column_index * local_cols, local_cols)
    increment_terms = jnp.einsum(
        "k,kfrc->frc", weights_local, columns, precision=lax.Precision.HIGHEST
    )
    increment_total = lax.psum(increment_terms, "cols")
    increment = lax.dynamic_slice_in_dim(increment_total, column_index * piece_cols, piece_cols, 2)
    columns_low = columns.astype(jnp.bfloat16)
    shard_piece = lax.all_gather(columns_low, "cols", axis=0, tiled=True)
    transform_part = lax.dynamic_slice(
        transform_low, (0, column_index * local_cols), (shard_piece.shape[0], local_cols)
    )
    updated = jnp.einsum(
        "kj,kfrc->jfrc", transform_part, shard_piece, preferred_element_type=jnp.float32
    )
    return (mean_now + increment, updated)


def solution(mesh):
    return jax.shard_map(
        local,
        mesh=mesh,
        in_specs=(
            P(None, "space", "cols"),
            P("cols", None, "space", None),
            P(),
            P("space"),
            P("space"),
            P("space"),
        ),
        out_specs=(P(None, "space", "cols"), P("cols", None, "space", None)),
        check_vma=False,
    )
```

profile of v0, /device:TPU:33, one launch (start us, length us, event | category | flops | bytes accessed | tf_op | source)
XLA Modules:
  0.0 870.6 jit_solution(11789694956395223728)
XLA Ops:
  10.8 3.6 collective-permute-start
  18.9 4.7 collective-permute-start.16
  26.1 4.0 collective-permute-start.2
  36.6 3.4 collective-permute-start.4
  40.2 16.9 %all_gather.21 = f32[6,18,256]{1,0,2:T(8,128)S(1)} all-gather(f32[6,18,32]{1,0,2:T(8,128)S(1)} %stack.286), channel_id=1, replica_groups=mesh['cols'=8,'space'=32] {'cols'}, dimensions={2}, use_global_device_ids=true | all-gather | bytes 124416 | tf_op jit(solution)/shard_map/all_gather | solution.py:121
  58.9 4.0 collective-permute-start.6
  72.4 16.9 %all_gather.22 = f32[6,18,256]{1,0,2:T(8,128)S(1)} all-gather(f32[6,18,32]{1,0,2:T(8,128)S(1)} %copy.157), channel_id=1, replica_groups=mesh['cols'=8,'space'=32] {'cols'}, dimensions={2}, use_global_device_ids=true | all-gather | bytes 124416 | tf_op jit(solution)/shard_map/all_gather | solution.py:121
  91.1 5.0 collective-permute-start.10
  103.1 4.0 collective-permute-start.12
  107.3 16.8 %all_gather.23 = f32[6,18,256]{1,0,2:T(8,128)S(1)} all-gather(f32[6,18,32]{1,0,2:T(8,128)S(1)} %copy.159), channel_id=1, replica_groups=mesh['cols'=8,'space'=32] {'cols'}, dimensions={2}, use_global_device_ids=true | all-gather | bytes 124416 | tf_op jit(solution)/shard_map/all_gather | solution.py:121
  125.9 10.2 %collective-permute-start.14 = (f32[6,2,36]{1,2,0:T(8,128)S(1)}, f32[6,2,36]{1,2,0:T(8,128)S(1)}, u32[]{:S(2)}, u32[]{:S(2)}) collective-permute-start(f32[6,2,36]{1,2,0:T(8,128)S(1)} %get-tuple-element.190), channel_id=1, source_target_pairs={{0,1},{1,2},{2,3},{3,4},{4,5},{5,6},{6,7},{7,8},{8,9},{9,10},{10,1... | collective-permute-start | bytes 5192 | tf_op jit(solution)/shard_map/ppermute | solution.py:22
  147.0 12.1 %collective-permute-start.18 = (f32[16,6,2,256]{3,0,2,1:T(8,128)S(1)}, f32[16,6,2,256]{3,0,2,1:T(8,128)S(1)}, u32[]{:S(2)}, u32[]{:S(2)}) collective-permute-start(f32[16,6,2,256]{3,0,2,1:T(8,128)S(1)} %get-tuple-element.138), channel_id=1, source_target_pairs={{0,1},{1,2},{2,3},{3,4},{4,5},{5,6},{6,7},{7,8},{8,9},{9,10},{10,1... | collective-permute-start | bytes 589832 | tf_op jit(solution)/shard_map/ppermute | solution.py:22
  168.4 12.6 %collective-permute-start.20 = (f32[16,6,2,256]{3,0,2,1:T(8,128)S(1)}, f32[16,6,2,256]{3,0,2,1:T(8,128)S(1)}, u32[]{:S(2)}, u32[]{:S(2)}) collective-permute-start(f32[16,6,2,256]{3,0,2,1:T(8,128)S(1)} %get-tuple-element.136), channel_id=1, source_target_pairs={{0,1},{1,2},{2,3},{3,4},{4,5},{5,6},{6,7},{7,8},{8,9},{9,10},{10,1... | collective-permute-start | bytes 589832 | tf_op jit(solution)/shard_map/ppermute | solution.py:22
  189.6 11.9 %collective-permute-start.22 = (f32[16,6,2,256]{3,0,2,1:T(8,128)S(1)}, f32[16,6,2,256]{3,0,2,1:T(8,128)S(1)}, u32[]{:S(2)}, u32[]{:S(2)}) collective-permute-start(f32[16,6,2,256]{3,0,2,1:T(8,128)S(1)} %get-tuple-element.134), channel_id=1, source_target_pairs={{0,1},{1,2},{2,3},{3,4},{4,5},{5,6},{6,7},{7,8},{8,9},{9,10},{10,1... | collective-permute-start | bytes 589832 | tf_op jit(solution)/shard_map/ppermute | solution.py:22
  201.7 22.8 %all_gather.24 = f32[6,18,256]{1,0,2:T(8,128)S(1)} all-gather(f32[6,18,32]{1,0,2:T(8,128)S(1)} %copy.161), channel_id=1, replica_groups=mesh['cols'=8,'space'=32] {'cols'}, dimensions={2}, use_global_device_ids=true | all-gather | bytes 124416 | tf_op jit(solution)/shard_map/all_gather | solution.py:121
  224.8 17.7 %all-gather = f32[8,32,16]{1,2,0:T(8,128)S(1)} all-gather(f32[1,32,16]{1,2,0:T(8,128)S(1)} %copy.167), channel_id=1, replica_groups=mesh['cols'=8,'space'=32] {'cols'}, dimensions={0}, use_global_device_ids=true | all-gather | bytes 18432 | tf_op jit(solution)/shard_map/all_gather | solution.py:123
  253.7 14.0 %all_gather.25 = f32[128,128]{1,0:T(8,128)S(1)} all-gather(f32[16,128]{1,0:T(8,128)S(1)} %copy.165), channel_id=1, replica_groups=mesh['cols'=8,'space'=32] {'cols'}, dimensions={0}, use_global_device_ids=true | all-gather | bytes 73728 | tf_op jit(solution)/shard_map/all_gather | solution.py:128
  270.4 113.3 %psum.22 = f32[128]{0:T(128)S(1)} all-reduce(f32[128]{0:T(128)S(1)} %convolution_bitcast_fusion.2), channel_id=1, replica_groups=mesh['cols'=8,'space'=32] {'space'}, use_global_device_ids=true, to_apply=%region_3.4 | all-reduce | flops 128 | bytes 1024 | tf_op jit(solution)/shard_map/psum | solution.py:135
  383.7 293.7 %all-reduce.12.cloned.1.call-done = f32[128,128]{1,0:T(8,128)} async-done(((f32[128,128]{1,0:T(8,128)}), f32[128,128]{1,0:T(8,128)}) %all-reduce.12.cloned.1.call-update) | async-done | bytes 65552 | tf_op jit(solution)/shard_map/psum | solution.py:135
  679.2 11.7 %cholesky.18 = f32[128,128]{1,0:T(8,128)S(1)} custom-call(f32[128,128]{1,0:T(8,128)S(1)} %fusion.170), custom_call_target="Cholesky" | custom-call | tf_op jit(solution)/shard_map/cholesky | solution.py:138
  692.3 9.8 %custom-call.9 = f32[1,128,128]{1,2,0:T(8,128)S(1)} custom-call(f32[1,128,128]{2,1,0:T(8,128)S(1)} %fusion.165), custom_call_target="InvertDiagBlocksLowerTriangular" | custom-call | tf_op jit(solution)/shard_map/triangular_solve | solution.py:140
  706.3 72.6 %all-reduce.14.cloned.1.call-done = f32[6,16,256]{1,2,0:T(8,128)} async-done(((f32[6,16,256]{1,2,0:T(8,128)}), f32[6,16,256]{1,2,0:T(8,128)}) %all-reduce.14.cloned.1.call-update) | async-done | bytes 98320 | tf_op jit(solution)/shard_map/psum | solution.py:149
  780.6 77.7 %all-gather.3.cloned.1.call-done = bf16[128,6,16,256]{3,0,2,1:T(8,128)(2,1)} async-done(((bf16[16,6,16,256]{3,0,2,1:T(8,128)(2,1)}), bf16[128,6,16,256]{3,0,2,1:T(8,128)(2,1)}) %all-gather.3.cloned.1.call-update) | async-done | bytes 6291472 | tf_op jit(solution)/shard_map/all_gather | solution.py:152
  858.3 3.7 fusion.362
  (273 shorter events, 92.5 us)
Async XLA Ops:
  7.2 670.2 %all-reduce.12.cloned.1.call-start = ((), (), s32[]{:S(2)}) async-start(), calls=%async_computation | async-start | bytes 131072 | tf_op jit(solution)/shard_map/psum | solution.py:135
  8.2 16.3 %collective-permute-start.1 = (f32[6,16,2]{2,1,0:T(8,128)S(1)}, f32[6,16,2]{2,1,0:T(8,128)S(1)}, u32[]{:S(2)}, u32[]{:S(2)}) collective-permute-start(f32[6,16,2]{2,1,0:T(8,128)S(1)} %get-tuple-element.229), channel_id=1, source_target_pairs={{32,0},{64,32},{96,64},{128,96},{160,128},{192,160},{224,192},{33,... | collective-permute-start | bytes 2312 | tf_op jit(solution)/shard_map/ppermute | solution.py:25
  10.8 13.7 %collective-permute-start = (f32[6,16,2]{2,1,0:T(8,128)S(1)}, f32[6,16,2]{2,1,0:T(8,128)S(1)}, u32[]{:S(2)}, u32[]{:S(2)}) collective-permute-start(f32[6,16,2]{2,1,0:T(8,128)S(1)} %get-tuple-element.228), channel_id=1, source_target_pairs={{0,32},{32,64},{64,96},{96,128},{128,160},{160,192},{192,224},{1,3... | collective-permute-start | bytes 2312 | tf_op jit(solution)/shard_map/ppermute | solution.py:22
  17.5 122.4 %collective-permute-start.17 = (f32[16,6,2,256]{3,0,2,1:T(8,128)}, f32[16,6,2,256]{3,0,2,1:T(8,128)}, u32[]{:S(2)}, u32[]{:S(2)}) collective-permute-start(f32[16,6,2,256]{3,0,2,1:T(8,128)} %get-tuple-element.141), channel_id=1, source_target_pairs={{1,0},{2,1},{3,2},{4,3},{5,4},{6,5},{7,6},{8,7},{9,8},{10,9},{11,1... | collective-permute-start | bytes 589832 | tf_op jit(solution)/shard_map/ppermute | solution.py:25
  18.9 121.0 %collective-permute-start.16 = (f32[16,6,2,256]{3,0,2,1:T(8,128)}, f32[16,6,2,256]{3,0,2,1:T(8,128)}, u32[]{:S(2)}, u32[]{:S(2)}) collective-permute-start(f32[16,6,2,256]{3,0,2,1:T(8,128)} %get-tuple-element.140), channel_id=1, source_target_pairs={{0,1},{1,2},{2,3},{3,4},{4,5},{5,6},{6,7},{7,8},{8,9},{9,10},{10,1... | collective-permute-start | bytes 589832 | tf_op jit(solution)/shard_map/ppermute | solution.py:22
  24.8 7.2 collective-permute-start.3
  34.0 23.4 %collective-permute-start.5 = (f32[6,16,2]{1,2,0:T(2,128)S(1)}, f32[6,16,2]{1,2,0:T(2,128)S(1)}, u32[]{:S(2)}, u32[]{:S(2)}) collective-permute-start(f32[6,16,2]{1,2,0:T(2,128)S(1)} %get-tuple-element.227), channel_id=1, source_target_pairs={{32,0},{64,32},{96,64},{128,96},{160,128},{192,160},{224,192},{33,... | collective-permute-start | bytes 2312 | tf_op jit(solution)/shard_map/ppermute | solution.py:25
  36.6 20.8 %collective-permute-start.4 = (f32[6,16,2]{1,2,0:T(2,128)S(1)}, f32[6,16,2]{1,2,0:T(2,128)S(1)}, u32[]{:S(2)}, u32[]{:S(2)}) collective-permute-start(f32[6,16,2]{1,2,0:T(2,128)S(1)} %get-tuple-element.226), channel_id=1, source_target_pairs={{0,32},{32,64},{64,96},{96,128},{128,160},{160,192},{192,224},{1,3... | collective-permute-start | bytes 2312 | tf_op jit(solution)/shard_map/ppermute | solution.py:22
  66.7 22.9 %collective-permute-start.9 = (f32[6,16,2]{1,2,0:T(2,128)}, f32[6,16,2]{1,2,0:T(2,128)S(1)}, u32[]{:S(2)}, u32[]{:S(2)}) collective-permute-start(f32[6,16,2]{1,2,0:T(2,128)} %get-tuple-element.225), channel_id=1, source_target_pairs={{32,0},{64,32},{96,64},{128,96},{160,128},{192,160},{224,192},{33,... | collective-permute-start | bytes 2312 | tf_op jit(solution)/shard_map/ppermute | solution.py:25
  69.9 19.8 %collective-permute-start.8 = (f32[6,16,2]{1,2,0:T(2,128)}, f32[6,16,2]{1,2,0:T(2,128)S(1)}, u32[]{:S(2)}, u32[]{:S(2)}) collective-permute-start(f32[6,16,2]{1,2,0:T(2,128)} %get-tuple-element.224), channel_id=1, source_target_pairs={{0,32},{32,64},{64,96},{96,128},{128,160},{160,192},{192,224},{1,3... | collective-permute-start | bytes 2312 | tf_op jit(solution)/shard_map/ppermute | solution.py:22
  89.8 7.9 collective-permute-start.11
  91.1 7.6 collective-permute-start.10
  100.2 24.2 %collective-permute-start.13 = (f32[6,16,2]{1,2,0:T(2,128)}, f32[6,16,2]{1,2,0:T(2,128)S(1)}, u32[]{:S(2)}, u32[]{:S(2)}) collective-permute-start(f32[6,16,2]{1,2,0:T(2,128)} %get-tuple-element.223), channel_id=1, source_target_pairs={{32,0},{64,32},{96,64},{128,96},{160,128},{192,160},{224,192},{33,... | collective-permute-start | bytes 2312 | tf_op jit(solution)/shard_map/ppermute | solution.py:25
  103.1 21.3 %collective-permute-start.12 = (f32[6,16,2]{1,2,0:T(2,128)}, f32[6,16,2]{1,2,0:T(2,128)S(1)}, u32[]{:S(2)}, u32[]{:S(2)}) collective-permute-start(f32[6,16,2]{1,2,0:T(2,128)} %get-tuple-element.222), channel_id=1, source_target_pairs={{0,32},{32,64},{64,96},{96,128},{128,160},{160,192},{192,224},{1,3... | collective-permute-start | bytes 2312 | tf_op jit(solution)/shard_map/ppermute | solution.py:22
  124.6 13.1 %collective-permute-start.15 = (f32[6,2,36]{1,2,0:T(8,128)S(1)}, f32[6,2,36]{1,2,0:T(8,128)S(1)}, u32[]{:S(2)}, u32[]{:S(2)}) collective-permute-start(f32[6,2,36]{1,2,0:T(8,128)S(1)} %get-tuple-element.191), channel_id=1, source_target_pairs={{1,0},{2,1},{3,2},{4,3},{5,4},{6,5},{7,6},{8,7},{9,8},{10,9},{11,1... | collective-permute-start | bytes 5192 | tf_op jit(solution)/shard_map/ppermute | solution.py:25
  125.9 12.7 %collective-permute-start.14 = (f32[6,2,36]{1,2,0:T(8,128)S(1)}, f32[6,2,36]{1,2,0:T(8,128)S(1)}, u32[]{:S(2)}, u32[]{:S(2)}) collective-permute-start(f32[6,2,36]{1,2,0:T(8,128)S(1)} %get-tuple-element.190), channel_id=1, source_target_pairs={{0,1},{1,2},{2,3},{3,4},{4,5},{5,6},{6,7},{7,8},{8,9},{9,10},{10,1... | collective-permute-start | bytes 5192 | tf_op jit(solution)/shard_map/ppermute | solution.py:22
  145.7 15.5 %collective-permute-start.19 = (f32[16,6,2,256]{3,0,2,1:T(8,128)S(1)}, f32[16,6,2,256]{3,0,2,1:T(8,128)S(1)}, u32[]{:S(2)}, u32[]{:S(2)}) collective-permute-start(f32[16,6,2,256]{3,0,2,1:T(8,128)S(1)} %get-tuple-element.139), channel_id=1, source_target_pairs={{1,0},{2,1},{3,2},{4,3},{5,4},{6,5},{7,6},{8,7},{9,8},{10,9},{11,1... | collective-permute-start | bytes 589832 | tf_op jit(solution)/shard_map/ppermute | solution.py:25
  147.0 15.1 %collective-permute-start.18 = (f32[16,6,2,256]{3,0,2,1:T(8,128)S(1)}, f32[16,6,2,256]{3,0,2,1:T(8,128)S(1)}, u32[]{:S(2)}, u32[]{:S(2)}) collective-permute-start(f32[16,6,2,256]{3,0,2,1:T(8,128)S(1)} %get-tuple-element.138), channel_id=1, source_target_pairs={{0,1},{1,2},{2,3},{3,4},{4,5},{5,6},{6,7},{7,8},{8,9},{9,10},{10,1... | collective-permute-start | bytes 589832 | tf_op jit(solution)/shard_map/ppermute | solution.py:22
  167.1 15.0 %collective-permute-start.21 = (f32[16,6,2,256]{3,0,2,1:T(8,128)S(1)}, f32[16,6,2,256]{3,0,2,1:T(8,128)S(1)}, u32[]{:S(2)}, u32[]{:S(2)}) collective-permute-start(f32[16,6,2,256]{3,0,2,1:T(8,128)S(1)} %get-tuple-element.137), channel_id=1, source_target_pairs={{1,0},{2,1},{3,2},{4,3},{5,4},{6,5},{7,6},{8,7},{9,8},{10,9},{11,1... | collective-permute-start | bytes 589832 | tf_op jit(solution)/shard_map/ppermute | solution.py:25
  168.4 15.2 %collective-permute-start.20 = (f32[16,6,2,256]{3,0,2,1:T(8,128)S(1)}, f32[16,6,2,256]{3,0,2,1:T(8,128)S(1)}, u32[]{:S(2)}, u32[]{:S(2)}) collective-permute-start(f32[16,6,2,256]{3,0,2,1:T(8,128)S(1)} %get-tuple-element.136), channel_id=1, source_target_pairs={{0,1},{1,2},{2,3},{3,4},{4,5},{5,6},{6,7},{7,8},{8,9},{9,10},{10,1... | collective-permute-start | bytes 589832 | tf_op jit(solution)/shard_map/ppermute | solution.py:22
  188.3 55.7 %collective-permute-start.23 = (f32[16,6,2,256]{3,0,2,1:T(8,128)}, f32[16,6,2,256]{3,0,2,1:T(8,128)S(1)}, u32[]{:S(2)}, u32[]{:S(2)}) collective-permute-start(f32[16,6,2,256]{3,0,2,1:T(8,128)} %get-tuple-element.135), channel_id=1, source_target_pairs={{1,0},{2,1},{3,2},{4,3},{5,4},{6,5},{7,6},{8,7},{9,8},{10,9},{11,1... | collective-permute-start | bytes 589832 | tf_op jit(solution)/shard_map/ppermute | solution.py:25
  189.6 54.4 %collective-permute-start.22 = (f32[16,6,2,256]{3,0,2,1:T(8,128)S(1)}, f32[16,6,2,256]{3,0,2,1:T(8,128)S(1)}, u32[]{:S(2)}, u32[]{:S(2)}) collective-permute-start(f32[16,6,2,256]{3,0,2,1:T(8,128)S(1)} %get-tuple-element.134), channel_id=1, source_target_pairs={{0,1},{1,2},{2,3},{3,4},{4,5},{5,6},{6,7},{7,8},{8,9},{9,10},{10,1... | collective-permute-start | bytes 589832 | tf_op jit(solution)/shard_map/ppermute | solution.py:22
  268.6 510.4 %all-reduce.14.cloned.1.call-start = ((), (), s32[]{:S(2)}) async-start(), calls=%async_computation.1 | async-start | bytes 1572864 | tf_op jit(solution)/shard_map/psum | solution.py:149
  704.6 153.7 %all-gather.3.cloned.1.call-start = ((), (), s32[]{:S(2)}) async-start(), calls=%async_computation.2 | async-start | bytes 7077888 | tf_op jit(solution)/shard_map/all_gather | solution.py:152
  (30 other events, 253.6 us)
Sparse Core Ops, SparseCore 0:
  268.7 408.6 all-reduce.11
  704.7 74.2 all-reduce.13
  780.8 77.4 all-gather.2
where the time goes:
time: 874 us; the launch traced here: 871 us
  waiting for transfers between devices  457 us (52%)
  blocking collectives  218 us (25%)
  starting transfers between devices  99.6 us (11%)
  other arithmetic  46.8 us (5%)
  local copies, waits for them, and re-layouts  27.1 us (3%)
  between operations  15.1 us (2%)
    psum x1, waiting for transfers between devices, local(): gram_sum, target = lax.psum((products, target_part), 'space')  294 us
    psum x1, blocking collectives, local(): gram_sum, target = lax.psum((products, target_part), 'space')  113 us
    ppermute x12, starting transfers between devices, padded_2(): lax.ppermute(lax.slice_in_dim(block, block.shape[dim] - width, None, axis...  77.8 us
    all_gather x1, waiting for transfers between devices, local(): shard_piece = lax.all_gather(columns_low, 'cols', axis=0, tiled=True)  77.7 us
    all_gather x4, blocking collectives, local(): carried = lax.all_gather(carried, 'cols', axis=2, tiled=True)  73.4 us
    psum x1, waiting for transfers between devices, local(): increment_total = lax.psum(increment_terms, 'cols')  72.6 us
    ppermute x12, starting transfers between devices, padded_2(): lax.ppermute(lax.slice_in_dim(block, 0, width, axis=dim), axis, backward)  21.6 us
    all_gather x1, blocking collectives, local(): lax.all_gather(mean_now[0] + mean_now[3], 'cols', axis=1, tiled=True)  17.7 us
  transfers between devices with their start and end apart: 27, of which 15 were waited for; matrix products, arithmetic and copies ran while one was open for 2% of the time, Pallas kernels for 0%

commit v1 on v0

v1 whole, which is shorter than its diff:
```python
import functools

import jax
import jax.numpy as jnp
from jax import lax
from jax.experimental import pallas as pl
from jax.experimental.pallas import tpu as pltpu
from jax.sharding import PartitionSpec as P

STEPS = 4
HALO = 8
TILE = 16
WIN = TILE + 2 * HALO
NC = 8
NS = 32
NCOL = 16
KALL = 128
WIDTH = 256
FR = 96
PIECE = 12
OBS = 128

HIGH = lax.Precision.HIGHEST
MESH = pl.DeviceIdType.MESH
ANY = pl.BlockSpec(memory_space=pl.ANY)
VMEM = pl.BlockSpec(memory_space=pltpu.VMEM)


def peer(c, s):
    return {"cols": c, "space": s}


def greet(peers):
    barrier = pltpu.get_barrier_semaphore()
    for device in peers:
        pl.semaphore_signal(barrier, inc=1, device_id=device, device_id_type=MESH)
    pl.semaphore_wait(barrier, len(peers))


def remote(src, dst, send, recv, device):
    return pltpu.make_async_remote_copy(
        src_ref=src, dst_ref=dst, send_sem=send, recv_sem=recv, device_id=device, device_id_type=MESH
    )


def halo_kernel(
    top_ref, bottom_ref, piece_ref, above_ref, below_ref, mean_ref, halo_send, halo_recv, mean_send, mean_recv, own_sem
):
    c = lax.axis_index("cols")
    s = lax.axis_index("space")
    down, up = lax.rem(s + 1, NS), lax.rem(s + NS - 1, NS)
    others = [lax.rem(c + i, NC) for i in range(1, NC)]
    targets = [(o, s, 1) for o in others]
    for o in [c] + others:
        targets += [(o, down, 0), (o, up, 2)]
    greet([peer(o, t) for o, t, _ in targets])
    own = pltpu.make_async_copy(piece_ref, mean_ref.at[1, c], own_sem)
    own.start()
    to_down = remote(bottom_ref, above_ref, halo_send.at[0], halo_recv.at[0], peer(c, down))
    to_up = remote(top_ref, below_ref, halo_send.at[1], halo_recv.at[1], peer(c, up))
    copies = []
    for i, (o, t, slot) in enumerate(targets):
        copies.append(
            remote(piece_ref, mean_ref.at[slot, c], mean_send.at[i], mean_recv.at[slot, c], peer(o, t))
        )
        copies[-1].start()
    to_down.start()
    to_up.start()
    for slot in range(3):
        for o in others if slot == 1 else [c] + others:
            remote(
                piece_ref, mean_ref.at[slot, o], mean_send.at[0], mean_recv.at[slot, o], peer(o, down)
            ).wait_recv()
    for copy in copies:
        copy.wait_send()
    own.wait()
    to_down.wait()
    to_up.wait()


def halo_exchange(top, bottom, piece):
    return pl.pallas_call(
        halo_kernel,
        out_shape=(
            jax.ShapeDtypeStruct(bottom.shape, bottom.dtype),
            jax.ShapeDtypeStruct(top.shape, top.dtype),
            jax.ShapeDtypeStruct((3, NC) + piece.shape, piece.dtype),
        ),
        in_specs=[ANY] * 3,
        out_specs=(ANY,) * 3,
        scratch_shapes=[
            pltpu.SemaphoreType.DMA((2,)),
            pltpu.SemaphoreType.DMA((2,)),
            pltpu.SemaphoreType.DMA((3 * NC - 1,)),
            pltpu.SemaphoreType.DMA((3, NC)),
            pltpu.SemaphoreType.DMA,
        ],
        compiler_params=pltpu.CompilerParams(collective_id=0, has_side_effects=True),
        name="halo_exchange",
    )(top, bottom, piece)


def row_difference(a):
    rows = a.shape[0]
    return pltpu.roll(a, rows - 1, 0) - pltpu.roll(a, 1, 0)


def col_difference(a, first, last):
    width = a.shape[1]
    after = jnp.where(last, 0.0, pltpu.roll(a, width - 1, 1))
    before = jnp.where(first, 0.0, pltpu.roll(a, 1, 1))
    return after - before


def new_velocities(fields, wet, first, last):
    top_pressure = fields[0] + fields[3]
    pressures = (top_pressure, top_pressure - 0.125 * fields[0])
    pairs = []
    for layer in range(2):
        u, v = fields[3 * layer + 1], fields[3 * layer + 2]
        p = pressures[layer]
        u_new = wet * (0.975 * u + 0.15 * v - 0.25 * row_difference(p))
        v_new = wet * (0.975 * v - 0.15 * u - 0.25 * col_difference(p, first, last))
        pairs.append((u_new, v_new))
    return pairs


def forecast_kernel(
    cov_ref,
    above_ref,
    below_ref,
    mean_ref,
    wet_ref,
    inside_ref,
    row_ref,
    col_ref,
    weight_ref,
    observed_ref,
    columns_ref,
    sensed_ref,
    meanf_ref,
    carried,
    held,
    surface,
    per_step,
):
    grid_step = pl.program_id(0)
    lane = lax.broadcasted_iota(jnp.int32, (WIN, WIDTH), 1)
    first, last = lane == 0, lane == WIDTH - 1
    wet = wet_ref[...]
    inside = inside_ref[...]

    @pl.when(grid_step == 0)
    def _():
        fields = [mean_ref[f] * inside for f in range(6)]
        for step in range(STEPS):
            pairs = new_velocities(fields, wet, first, last)
            after = []
            for layer in range(2):
                h = fields[3 * layer]
                depth = (1.0, 2.0)[layer] + h
                u, v = pairs[layer]
                base = 6 * step + 3 * layer
                carried[base] = depth
                carried[base + 1] = u
                carried[base + 2] = v
                h_new = inside * (h - 0.25 * (row_difference(depth * u) + col_difference(depth * v, first, last)))
                after += [h_new, u, v]
            fields = after
        for f in range(6):
            meanf_ref[pl.ds(TILE * f, TILE)] = fields[f][HALO : HALO + TILE]
        surface[pl.ds(NCOL * TILE, TILE)] = (fields[0] + fields[3])[HALO : HALO + TILE]

    for i in range(per_step):
        k = grid_step * per_step + i
        above = above_ref[i].astype(jnp.float32)
        below = below_ref[i].astype(jnp.float32)
        fields = []
        for f in range(6):
            rows = jnp.concatenate(
                [
                    above[HALO * f : HALO * (f + 1)],
                    cov_ref[i, pl.ds(TILE * f, TILE)],
                    below[HALO * f : HALO * (f + 1)],
                ],
                axis=0,
            )
            fields.append(rows * inside)
        for step in range(STEPS):
            pairs = new_velocities(fields, wet, first, last)
            after = []
            for layer in range(2):
                h = fields[3 * layer]
                u, v = pairs[layer]
                base = 6 * step + 3 * layer
                depth = carried[base]
                rows_flux = depth * u + h * carried[base + 1]
                cols_flux = depth * v + h * carried[base + 2]
                h_new = inside * (h - 0.25 * (row_difference(rows_flux) + col_difference(cols_flux, first, last)))
                after += [h_new, u, v]
            fields = after
        for f in range(6):
            at = pl.ds(pl.multiple_of(k * FR + TILE * f, TILE), TILE)
            for half in range(2):
                held[half, at] = fields[f][HALO : HALO + TILE, 128 * half : 128 * (half + 1)]
        surface[pl.ds(pl.multiple_of(k * TILE, TILE), TILE)] = (fields[0] + fields[3])[HALO : HALO + TILE]

    @pl.when(grid_step == pl.num_programs(0) - 1)
    def _():
        cells = lax.broadcasted_iota(jnp.int32, (WIDTH, OBS), 0)
        pick = (cells == col_ref[...]).astype(jnp.float32)
        at_rows = lax.broadcasted_iota(jnp.int32, (TILE, OBS), 0) == row_ref[...]
        picked = jnp.dot(surface[...], pick, precision=HIGH, preferred_element_type=jnp.float32)
        picked = picked.reshape(NCOL + 1, TILE, OBS)
        values = jnp.sum(jnp.where(at_rows[None], picked, 0.0), axis=1)
        weight = weight_ref[...]
        sensed_ref[pl.ds(0, NCOL)] = values[:NCOL] * weight
        innovation = weight * (observed_ref[...] - values[NCOL:])
        below_first = lax.broadcasted_iota(jnp.int32, (8, OBS), 0) > 0
        sensed_ref[pl.ds(NCOL, 8)] = jnp.where(below_first, 0.0, jnp.broadcast_to(innovation, (8, OBS)))

        def gather_row(fr, carry):
            for half in range(2):
                value = held[half, pl.ds(fr, NCOL, stride=FR)]
                columns_ref[fr, :, 128 * half : 128 * (half + 1)] = value.astype(jnp.bfloat16)
            return carry

        lax.fori_loop(0, FR, gather_row, 0, unroll=8)


def forecast(cov, above, below, mean, wet, inside, row, col, weight, observed):
    per_step = 2
    block = lambda rows: pl.BlockSpec((per_step, rows, WIDTH), lambda i: (i, 0, 0))
    whole = lambda shape: pl.BlockSpec(shape, lambda i: (0,) * len(shape))
    return pl.pallas_call(
        functools.partial(forecast_kernel, per_step=per_step),
        grid=(NCOL // per_step,),
        out_shape=(
            jax.ShapeDtypeStruct((FR, NCOL, WIDTH), jnp.bfloat16),
            jax.ShapeDtypeStruct((NCOL + 8, OBS), jnp.float32),
            jax.ShapeDtypeStruct((FR, WIDTH), jnp.float32),
        ),
        in_specs=[
            block(FR),
            block(6 * HALO),
            block(6 * HALO),
            whole((6, WIN, WIDTH)),
            whole((WIN, WIDTH)),
            whole((WIN, WIDTH)),
            whole((1, OBS)),
            whole((1, OBS)),
            whole((1, OBS)),
            whole((1, OBS)),
        ],
        out_specs=(whole((FR, NCOL, WIDTH)), whole((NCOL + 8, OBS)), whole((FR, WIDTH))),
        scratch_shapes=[
            pltpu.VMEM((6 * STEPS, WIN, WIDTH), jnp.float32),
            pltpu.VMEM((2, NCOL * FR, 128), jnp.float32),
            pltpu.VMEM(((NCOL + 1) * TILE, WIDTH), jnp.float32),
        ],
        compiler_params=pltpu.CompilerParams(vmem_limit_bytes=40 * 1024 * 1024),
        name="forecast",
    )(cov, above, below, mean, wet, inside, row, col, weight, observed)


def gram_kernel(
    columns_ref, sensed_ref, cells_ref, gram_ref, right, block, across, layers,
    send_a, recv_a, send_b, recv_b, send_c, recv_c, send_d, recv_d, own_sem,
):
    c = lax.axis_index("cols")
    s = lax.axis_index("space")
    y, zh, x = s // 8, lax.rem(s // 4, 2), lax.rem(s, 4)
    plane = y * 4 + x
    others = [lax.rem(c + i, NC) for i in range(1, NC)]
    planes = [lax.rem(plane + i, 16) for i in range(1, 16)]
    space_of = lambda p: (p // 4) * 8 + zh * 4 + lax.rem(p, 4)
    far = y * 8 + (1 - zh) * 4 + x
    line = [(o, s, zh * NC + o) for o in others] + [(o, far, (1 - zh) * NC + o) for o in [c] + others]
    greet([peer(o, t) for o, t, _ in line] + [peer(c, space_of(p)) for p in planes])

    own_rows = pl.ds(pl.multiple_of(c * NCOL, NCOL), NCOL)
    mine = sensed_ref.at[pl.ds(0, NCOL)]
    first = []
    for i, o in enumerate(others):
        copy = remote(mine, right.at[own_rows], send_a.at[i], recv_a.at[c], peer(o, s))
        copy.start()
        first.append(copy)
    bulk = []
    for i, o in enumerate(others):
        source = columns_ref.at[pl.ds(o * PIECE, PIECE)]
        copy = remote(source, cells_ref.at[:, own_rows], send_d.at[i], recv_d.at[c], peer(o, s))
        copy.start()
        bulk.append(copy)
    own = pltpu.make_async_copy(columns_ref.at[pl.ds(c * PIECE, PIECE)], cells_ref.at[:, own_rows], own_sem)
    own.start()

    right[own_rows] = sensed_ref[pl.ds(0, NCOL)]
    right[pl.ds(KALL, 8)] = sensed_ref[pl.ds(NCOL, 8)]
    right[pl.ds(KALL + 8, KALL - 8)] = jnp.zeros((KALL - 8, OBS), jnp.float32)
    for o in others:
        rows = pl.ds(pl.multiple_of(o * NCOL, NCOL), NCOL)
        remote(mine, right.at[rows], send_a.at[0], recv_a.at[o], peer(o, s)).wait_recv()
    part = lax.dot_general(
        sensed_ref[pl.ds(0, NCOL)], right[...], (((1,), (1,)), ((), ())),
        precision=HIGH, preferred_element_type=jnp.float32,
    )
    block[...] = part
    second = []
    for i, p in enumerate(planes):
        copy = remote(block, across.at[plane], send_b.at[i], recv_b.at[plane], peer(c, space_of(p)))
        copy.start()
        second.append(copy)
    across[plane] = part
    for p in planes:
        remote(block, across.at[p], send_b.at[0], recv_b.at[p], peer(c, space_of(p))).wait_recv()
    total = across[0]
    for p in range(1, 16):
        total = total + across[p]
    place = zh * NC + c
    layers[place] = total
    third = []
    for i, (o, t, _) in enumerate(line):
        copy = remote(layers.at[place], layers.at[place], send_c.at[i], recv_c.at[place], peer(o, t))
        copy.start()
        third.append(copy)
    for o, t, slot in line:
        remote(layers.at[slot], layers.at[slot], send_c.at[0], recv_c.at[slot], peer(o, t)).wait_recv()
    for o in range(NC):
        gram_ref[pl.ds(o * NCOL, NCOL)] = layers[o] + layers[NC + o]
    for o in others:
        rows = pl.ds(pl.multiple_of(o * NCOL, NCOL), NCOL)
        source = columns_ref.at[pl.ds(0, PIECE)]
        remote(source, cells_ref.at[:, rows], send_d.at[0], recv_d.at[o], peer(o, s)).wait_recv()
    own.wait()
    for copy in first + second + third + bulk:
        copy.wait_send()


def gram_exchange(columns, sensed):
    dma = pltpu.SemaphoreType.DMA
    return pl.pallas_call(
        gram_kernel,
        out_shape=(
            jax.ShapeDtypeStruct((PIECE, KALL, WIDTH), jnp.bfloat16),
            jax.ShapeDtypeStruct((KALL, 2 * KALL), jnp.float32),
        ),
        in_specs=[ANY, VMEM],
        out_specs=(ANY, VMEM),
        scratch_shapes=[
            pltpu.VMEM((2 * KALL, OBS), jnp.float32),
            pltpu.VMEM((NCOL, 2 * KALL), jnp.float32),
            pltpu.VMEM((16, NCOL, 2 * KALL), jnp.float32),
            pltpu.VMEM((2 * NC, NCOL, 2 * KALL), jnp.float32),
            dma((NC - 1,)),
            dma((NC,)),
            dma((15,)),
            dma((16,)),
            dma((15,)),
            dma((16,)),
            dma((NC - 1,)),
            dma((NC,)),
            dma,
        ],
        compiler_params=pltpu.CompilerParams(collective_id=1, has_side_effects=True),
        name="gram_exchange",
    )(columns, sensed)


def transform_kernel(
    transform_ref, weights_ref, cells_ref, result_ref, increment_ref, made, added,
    send_a, recv_a, send_b, recv_b, own_sems,
):
    c = lax.axis_index("cols")
    s = lax.axis_index("space")
    others = [lax.rem(c + i, NC) for i in range(1, NC)]
    greet([peer(o, s) for o in others])
    transform = transform_ref[...]
    weights = weights_ref[...]
    for fr in range(PIECE):
        cell = cells_ref[fr]
        out = jnp.dot(transform, cell, preferred_element_type=jnp.float32)
        made[fr] = out.astype(jnp.bfloat16)
        row = jnp.dot(weights, cell.astype(jnp.float32), precision=HIGH, preferred_element_type=jnp.float32)
        added[fr] = row
    copies = []
    mine = pl.ds(c * PIECE, PIECE)
    for i, o in enumerate(others):
        rows = pl.ds(pl.multiple_of(o * NCOL, NCOL), NCOL)
        copies.append(
            remote(made.at[:, rows], result_ref.at[mine], send_a.at[i], recv_a.at[c], peer(o, s))
        )
        copies.append(remote(added, increment_ref.at[c], send_b.at[i], recv_b.at[c], peer(o, s)))
    for copy in copies:
        copy.start()
    own_rows = pl.ds(pl.multiple_of(c * NCOL, NCOL), NCOL)
    own = pltpu.make_async_copy(made.at[:, own_rows], result_ref.at[mine], own_sems.at[0])
    own_added = pltpu.make_async_copy(added, increment_ref.at[c], own_sems.at[1])
    own.start()
    own_added.start()
    for o in others:
        theirs = result_ref.at[pl.ds(o * PIECE, PIECE)]
        remote(made.at[:, own_rows], theirs, send_a.at[0], recv_a.at[o], peer(o, s)).wait_recv()
        remote(added, increment_ref.at[o], send_b.at[0], recv_b.at[o], peer(o, s)).wait_recv()
    own.wait()
    own_added.wait()
    for copy in copies:
        copy.wait_send()


def transform_exchange(transform, weights, cells):
    dma = pltpu.SemaphoreType.DMA
    return pl.pallas_call(
        transform_kernel,
        out_shape=(
            jax.ShapeDtypeStruct((FR, NCOL, WIDTH), jnp.bfloat16),
            jax.ShapeDtypeStruct((NC, PIECE, 8, WIDTH), jnp.float32),
        ),
        in_specs=[VMEM] * 3,
        out_specs=(ANY, ANY),
        scratch_shapes=[
            pltpu.VMEM((PIECE, KALL, WIDTH), jnp.bfloat16),
            pltpu.VMEM((PIECE, 8, WIDTH), jnp.float32),
            dma((NC - 1,)),
            dma((NC,)),
            dma((NC - 1,)),
            dma((NC,)),
            dma((2,)),
        ],
        compiler_params=pltpu.CompilerParams(collective_id=2, has_side_effects=True),
        name="transform_exchange",
    )(transform, weights, cells)


def place_kernel(result_ref, out_ref, wide):
    for half in range(2):
        part = result_ref[:, :, 128 * half : 128 * (half + 1)].astype(jnp.float32)
        wide[half] = part.reshape(8 * NCOL, 128)
    for j in range(NCOL):
        for half in range(2):
            out_ref[j, :, 128 * half : 128 * (half + 1)] = wide[half, pl.ds(j, 8, stride=NCOL)]


def place(result):
    return pl.pallas_call(
        place_kernel,
        grid=(FR // 8,),
        out_shape=jax.ShapeDtypeStruct((NCOL, FR, WIDTH), jnp.float32),
        in_specs=[pl.BlockSpec((8, NCOL, WIDTH), lambda i: (i, 0, 0))],
        out_specs=pl.BlockSpec((NCOL, 8, WIDTH), lambda i: (0, i, 0)),
        scratch_shapes=[pltpu.VMEM((2, 8 * NCOL, 128), jnp.float32)],
        name="place",
    )(result)


def mean_windows(gathered):
    wide = gathered.reshape(3, NC, 6, TILE, WIDTH // NC).transpose(2, 0, 3, 1, 4).reshape(6, 3, TILE, WIDTH)
    return jnp.concatenate([wide[:, 0, TILE - HALO :], wide[:, 1], wide[:, 2, :HALO]], axis=1)


def local(mean_state, covariance, land_mask, stations, observed, obs_weight):
    s = lax.axis_index("space")
    c = lax.axis_index("cols")
    first_row = s * TILE
    top = covariance[:, :, :HALO].astype(jnp.bfloat16).reshape(NCOL, 6 * HALO, WIDTH)
    bottom = covariance[:, :, TILE - HALO :].astype(jnp.bfloat16).reshape(NCOL, 6 * HALO, WIDTH)
    piece = mean_state.reshape(-1, 128)
    above, below, gathered = halo_exchange(top, bottom, piece)
    pad = ((HALO, HALO), (0, 0))
    wet = lax.dynamic_slice_in_dim(jnp.pad(land_mask, pad), first_row, WIN, 0).astype(jnp.float32)
    grid_row = first_row - HALO + lax.broadcasted_iota(jnp.int32, (WIN, WIDTH), 0)
    inside = ((grid_row >= 0) & (grid_row < NS * TILE)).astype(jnp.float32)
    cell = stations - first_row * WIDTH
    columns, sensed, mean_forecast = forecast(
        covariance.reshape(NCOL, FR, WIDTH),
        above,
        below,
        mean_windows(gathered),
        wet,
        inside,
        (cell // WIDTH)[None],
        (cell % WIDTH)[None],
        obs_weight[None],
        observed[None],
    )
    cells, gram = gram_exchange(columns, sensed)
    identity = jnp.eye(KALL, dtype=jnp.float32)
    lower = lax.linalg.cholesky(identity + gram[:, :KALL])
    inverse = lax.linalg.triangular_solve(lower, identity, left_side=True, lower=True)
    halfway = jnp.dot(inverse, gram[:, KALL], precision=HIGH)
    weights = jnp.dot(halfway, inverse, precision=HIGH)
    result, increments = transform_exchange(
        inverse.astype(jnp.bfloat16), jnp.broadcast_to(weights[None], (8, KALL)), cells
    )
    updated = place(result).reshape(NCOL, 6, TILE, WIDTH)
    increment = increments[:, :, 0].reshape(FR, WIDTH)
    mean = (mean_forecast + increment).reshape(6, TILE, WIDTH)
    width = WIDTH // NC
    return lax.dynamic_slice_in_dim(mean, c * width, width, 2), updated


def solution(mesh):
    return jax.shard_map(
        local,
        mesh=mesh,
        in_specs=(
            P(None, "space", "cols"),
            P("cols", None, "space", None),
            P(),
            P("space"),
            P("space"),
            P("space"),
        ),
        out_specs=(P(None, "space", "cols"), P("cols", None, "space", None)),
        check_vma=False,
    )
```

time: 874 us -> 170 us (0.19)
  waiting for transfers between devices: 457 us -> 0 us
  blocking collectives: 218 us -> 0 us
  Pallas kernels: 0 us -> 129 us
  starting transfers between devices: 99.6 us -> 0 us
  other arithmetic: 46.8 us -> 26.2 us
  local copies, waits for them, and re-layouts: 27.1 us -> 11.7 us
  between operations: 15.1 us -> 0.89 us
    psum x2 -> x0, waiting for transfers between devices: 366 us -> none  [the longest x1 294 us: local(): gram_sum, target = lax.psum((products, target_part), 'space')]
    pallas_call x0 -> x5, Pallas kernels: none -> 129 us  [the longest x1 44.6 us: transform_exchange(): pl.pallas_call(transform_kernel, out_shape=(jax.ShapeDtypeStruct((FR, NCO...]
    psum x1 -> x0, blocking collectives: 113 us -> none  [local(): gram_sum, target = lax.psum((products, target_part), 'space')]
    all_gather x6 -> x0, blocking collectives: 105 us -> none  [the longest x4 73.4 us: local(): carried = lax.all_gather(carried, 'cols', axis=2, tiled=True)]
    ppermute x24 -> x0, starting transfers between devices: 99.5 us -> none  [the longest x12 77.8 us: padded_2(): lax.ppermute(lax.slice_in_dim(block, block.shape[dim] - width, None, axis...]
    all_gather x1 -> x0, waiting for transfers between devices: 77.7 us -> none  [local(): shard_piece = lax.all_gather(columns_low, 'cols', axis=0, tiled=True)]
    ppermute x24 -> x0, waiting for transfers between devices: 13.3 us -> none  [the longest x12 7.28 us: padded_2(): lax.ppermute(lax.slice_in_dim(block, 0, width, axis=dim), axis, backward)]
    unnamed x104 -> x20, local copies, waits for them, and re-layouts: 11 us -> 1.51 us
  transfers between devices with their start and end apart: 27 -> 0, of which waited for: 15 -> 0; matrix products, arithmetic and copies ran while one was open for 2% -> 0% of each run, Pallas kernels for 0% -> 0%
where the time goes in v1:
time: 170 us; the launch traced here: 169 us
  Pallas kernels  129 us (76%)
  other arithmetic  26.2 us (15%)
  local copies, waits for them, and re-layouts  11.7 us (7%)
    pallas_call x1, Pallas kernels, transform_exchange(): pl.pallas_call(transform_kernel, out_shape=(jax.ShapeDtypeStruct((FR, NCO...  44.6 us
    pallas_call x1, Pallas kernels, halo_exchange(): pl.pallas_call(halo_kernel, out_shape=(jax.ShapeDtypeStruct(bottom.shape,...  37.2 us
    pallas_call x1, Pallas kernels, gram_exchange(): pl.pallas_call(gram_kernel, out_shape=(jax.ShapeDtypeStruct((PIECE, KALL,...  29.8 us
    another operation x3, other arithmetic, local(): lower = lax.linalg.cholesky(identity + gram[:, :KALL])  12.4 us
    another operation x2, other arithmetic, local(): lax.linalg.triangular_solve(lower, identity, left_side=True, lower=True)  10.5 us
    pallas_call x1, Pallas kernels, forecast(): pl.pallas_call(functools.partial(forecast_kernel, per_step=per_step), gri...  10.4 us
    pallas_call x1, Pallas kernels, place(): pl.pallas_call(place_kernel, grid=(FR // 8,), out_shape=jax.ShapeDtypeStr...  7.17 us
    reshape x3, local copies, waits for them, and re-layouts, mean_windows(): gathered.reshape(3, NC, 6, TILE, WIDTH // NC).transpose(2, 0, 3, 1, 4)  4.72 us

profile of v1, /device:TPU:33, one launch (start us, length us, event | category | flops | bytes accessed | tf_op | source)
XLA Modules:
  0.0 169.1 jit_solution(15498626057261475919)
XLA Ops:
  0.6 1.5 convert.4
  2.2 0.9 slice_bitcast_fusion
  3.1 0.7 reshape.40.piece_ref
  3.8 37.2 %halo_exchange.1 = (bf16[16,48,256]{2,1,0:T(8,128)(2,1)}, bf16[16,48,256]{2,1,0:T(8,128)(2,1)}, f32[3,8,24,128]{3,2,1,0:T(8,128)}) custom-call(bf16[16,48,256]{2,1,0:T(8,128)(2,1)} %get-tuple-element.25.top_ref, bf16[16,48,256]{2,1,0:T(8,128)(2,1)} %get-tuple-element.24.bottom_ref, f32[24,128]{1,0:T(8,128)} %reshape.40.piece_ref), custom_call_target="tpu_custom_call" | custom-call | tf_op jit(solution)/shard_map/halo_exchange/pallas_call | solution.py:82
  41.0 1.2 reshape.41
  42.2 1.7 %copy.14 = f32[3,8,6,16,32]{4,1,3,2,0:T(8,128)} copy(f32[3,8,6,16,32]{4,3,2,1,0:T(8,128)S(1)} %reshape.41) | data formatting | bytes 589824 | tf_op jit(solution)/shard_map/reshape | solution.py:456
  44.0 1.8 %reshape.42 = f32[6,3,16,256]{3,2,0,1:T(8,128)S(1)} reshape(f32[6,3,16,8,32]{4,3,2,0,1:T(8,128)} %bitcast.53) | data formatting | bytes 589824 | tf_op jit(solution)/shard_map/reshape | solution.py:456
  46.0 10.4 %forecast.1 = (bf16[96,16,256]{2,1,0:T(8,128)(2,1)S(1)}, f32[24,128]{1,0:T(8,128)S(1)}, f32[96,256]{1,0:T(8,128)S(1)}) custom-call(f32[16,96,256]{2,1,0:T(8,128)S(1)} %bitcast.50, bf16[16,48,256]{2,1,0:T(8,128)(2,1)S(1)} %copy-done.2, bf16[16,48,256]{2,1,0:T(8,128)(2,1)S(1)} %copy-done.3, f32[6,32,256]{2,1,0:T(8,128)S(1)} %pad_maximum_fusion.mean_ref, ...), custom_call_target="tpu_custom_call" | custom-call | tf_op jit(solution)/shard_map/forecast/pallas_call | solution.py:235
  56.4 0.9 copy-done.1
  57.3 0.6 copy-done.4
  57.9 29.8 %gram_exchange.1 = (bf16[12,128,256]{2,1,0:T(8,128)(2,1)}, f32[128,256]{1,0:T(8,128)}) custom-call(bf16[96,16,256]{2,1,0:T(8,128)(2,1)} %copy-done.1, f32[24,128]{1,0:T(8,128)} %copy-done.4), custom_call_target="tpu_custom_call" | custom-call | tf_op jit(solution)/shard_map/gram_exchange/pallas_call | solution.py:341
  87.7 0.9 slice_add_fusion
  88.7 0.9 fusion.3
  89.6 11.7 %cholesky.18 = f32[128,128]{1,0:T(8,128)S(1)} custom-call(f32[128,128]{1,0:T(8,128)S(1)} %fusion.3), custom_call_target="Cholesky" | custom-call | tf_op jit(solution)/shard_map/cholesky | solution.py:487
  101.3 0.6 compare_reduce_fusion
  101.9 0.7 fusion
  102.6 9.8 %custom-call.5 = f32[1,128,128]{1,2,0:T(8,128)S(1)} custom-call(f32[1,128,128]{2,1,0:T(8,128)S(1)} %fusion), custom_call_target="InvertDiagBlocksLowerTriangular" | custom-call | tf_op jit(solution)/shard_map/triangular_solve | solution.py:488
  112.4 0.9 fusion.8
  113.3 0.9 slice_reduce_fusion.1
  114.6 0.6 broadcast_in_dim.23.weights_ref
  115.2 44.6 %transform_exchange.1 = (bf16[96,16,256]{2,1,0:T(8,128)(2,1)}, f32[8,12,8,256]{3,2,1,0:T(8,128)}) custom-call(bf16[128,128]{1,0:T(8,128)(2,1)} %get-tuple-element.28.transform_ref, f32[8,128]{1,0:T(8,128)} %broadcast_in_dim.23.weights_ref, bf16[12,128,256]{2,1,0:T(8,128)(2,1)} %get-tuple-element.19.cells_ref), custom_call_target="tpu_custom_call" | custom-call | tf_op jit(solution)/shard_map/transform_exchange/pallas_call | solution.py:412
  159.8 1.4 slice_reduce_fusion
  161.3 0.7 constant_dynamic-slice_fusion
  162.0 7.2 %place.1 = f32[16,96,256]{2,1,0:T(8,128)} custom-call(bf16[96,16,256]{2,1,0:T(8,128)(2,1)} %get-tuple-element.21.result_ref), custom_call_target="tpu_custom_call" | custom-call | tf_op jit(solution)/shard_map/place/pallas_call | solution.py:444
  (32 shorter events, 0.7 us)
Async XLA Ops:
  0.6 2.5 %copy-start.8 = (f32[6,16,32]{2,1,0:T(8,128)S(1)}, f32[6,16,32]{2,1,0:T(8,128)}, u32[]{:S(2)}) copy-start(f32[6,16,32]{2,1,0:T(8,128)} %param.6) | copy-start | bytes 36868
  42.2 3.6 %copy-start.7 = (s32[512,256]{1,0:T(8,128)S(1)}, s32[512,256]{1,0:T(8,128)}, u32[]{:S(2)}) copy-start(s32[512,256]{1,0:T(8,128)} %param.8) | copy-start | bytes 1572868
  43.9 2.0 %copy-start.9 = (s32[128]{0:T(128)S(1)}, s32[128]{0:T(128)}, u32[]{:S(2)}) copy-start(s32[128]{0:T(128)} %param.9) | copy-start | bytes 1540
  43.9 2.0 %copy-start = (f32[16,6,16,256]{3,2,1,0:T(8,128)S(1)}, f32[16,6,16,256]{3,2,1,0:T(8,128)}, u32[]{:S(2)}) copy-start(f32[16,6,16,256]{3,2,1,0:T(8,128)} %param.7) | copy-start | bytes 4718596
  43.9 2.0 %copy-start.2 = (bf16[16,48,256]{2,1,0:T(8,128)(2,1)S(1)}, bf16[16,48,256]{2,1,0:T(8,128)(2,1)}, u32[]{:S(2)}) copy-start(bf16[16,48,256]{2,1,0:T(8,128)(2,1)} %get-tuple-element.12.above_ref) | copy-start | bytes 1179652
  43.9 2.0 %copy-start.3 = (bf16[16,48,256]{2,1,0:T(8,128)(2,1)S(1)}, bf16[16,48,256]{2,1,0:T(8,128)(2,1)}, u32[]{:S(2)}) copy-start(bf16[16,48,256]{2,1,0:T(8,128)(2,1)} %get-tuple-element.13.below_ref) | copy-start | bytes 1179652
  44.0 2.0 %copy-start.5 = (f32[128]{0:T(128)S(1)}, f32[128]{0:T(128)}, u32[]{:S(2)}) copy-start(f32[128]{0:T(128)} %param.11) | copy-start | bytes 1540
  44.0 2.0 %copy-start.6 = (f32[128]{0:T(128)S(1)}, f32[128]{0:T(128)}, u32[]{:S(2)}) copy-start(f32[128]{0:T(128)} %param.10) | copy-start | bytes 1540
  56.4 0.9 copy-start.1
  57.3 0.6 copy-start.4

commit v2 on v0

v2 whole, which is shorter than its diff:
```python
import jax
import jax.numpy as jnp
from jax import lax
from jax.experimental import pallas as pl
from jax.experimental.pallas import tpu as pltpu
from jax.sharding import PartitionSpec as P

STEPS = 4
HALO = 8
TILE = 16
WIN = TILE + 2 * HALO
NC = 8
NS = 32
NCOL = 16
KALL = 128
WIDTH = 256
FR = 96
PIECE = 12
OBS = 128

HIGH = lax.Precision.HIGHEST
MESH = pl.DeviceIdType.MESH
ANY = pl.BlockSpec(memory_space=pl.ANY)
VMEM = pl.BlockSpec(memory_space=pltpu.VMEM)


def peer(c, s):
    return {"cols": c, "space": s}


def greet(peers):
    barrier = pltpu.get_barrier_semaphore()
    for device in peers:
        pl.semaphore_signal(barrier, inc=1, device_id=device, device_id_type=MESH)
    pl.semaphore_wait(barrier, len(peers))


def remote(src, dst, send, recv, device):
    return pltpu.make_async_remote_copy(
        src_ref=src, dst_ref=dst, send_sem=send, recv_sem=recv, device_id=device, device_id_type=MESH
    )


def row_difference(a):
    rows = a.shape[0]
    return pltpu.roll(a, rows - 1, 0) - pltpu.roll(a, 1, 0)


def col_difference(a, first, last):
    width = a.shape[1]
    after = jnp.where(last, 0.0, pltpu.roll(a, width - 1, 1))
    before = jnp.where(first, 0.0, pltpu.roll(a, 1, 1))
    return after - before


def new_velocities(fields, wet, first, last):
    top_pressure = fields[0] + fields[3]
    pressures = (top_pressure, top_pressure - 0.125 * fields[0])
    pairs = []
    for layer in range(2):
        u, v = fields[3 * layer + 1], fields[3 * layer + 2]
        p = pressures[layer]
        u_new = wet * (0.975 * u + 0.15 * v - 0.25 * row_difference(p))
        v_new = wet * (0.975 * v - 0.15 * u - 0.25 * col_difference(p, first, last))
        pairs.append((u_new, v_new))
    return pairs


BLOCK = 32


def factor(gram, stack):
    stack[...] = jnp.zeros(stack.shape, jnp.float32)
    row = lax.broadcasted_iota(jnp.int32, (BLOCK, KALL), 0)
    lane = lax.broadcasted_iota(jnp.int32, (BLOCK, KALL), 1)

    def one(b, carry):
        start = pl.multiple_of(b * BLOCK, BLOCK)
        back = lax.rem(KALL - start, KALL)
        done = stack[...]
        turned = pltpu.roll(done[:, :KALL], back, 1)
        product = lax.dot_general(
            turned, done, (((0,), (0,)), ((), ())), precision=HIGH, preferred_element_type=jnp.float32
        )[:BLOCK]
        eye = (lane == row + start).astype(jnp.float32)
        left = gram[pl.ds(start, BLOCK)] + eye - product[:, :KALL]
        right = eye - product[:, KALL:]
        square = pltpu.roll(left, back, 1)
        cols = [jnp.broadcast_to(square[:, m : m + 1], (BLOCK, KALL)) for m in range(BLOCK)]
        scale = jnp.zeros((BLOCK, KALL), jnp.float32)
        for j in range(BLOCK):
            r = lax.rsqrt(cols[j][j : j + 1])
            col = cols[j] * r
            strict = jnp.where(row > j, col, 0.0)
            for m in range(j + 1, BLOCK):
                cols[m] = cols[m] - strict * col[m : m + 1]
            left = left - strict * (left[j : j + 1] * r)
            right = right - strict * (right[j : j + 1] * r)
            scale = jnp.where(row == j, r, scale)
        stack[pl.ds(start, BLOCK), :KALL] = left * scale
        stack[pl.ds(start, BLOCK), KALL:] = right * scale
        return carry

    lax.fori_loop(0, KALL // BLOCK, one, 0)


CHUNKS = 8
PER = NCOL // CHUNKS
EDGE = PER * 6 * HALO
GROUPS = 4
GROUP = PIECE // GROUPS


def filter_kernel(
    cov_ref, piece_ref, land_ref, stations_ref, observed_ref, weight_ref,
    result_ref, increment_ref, meanf_ref,
    cov, wet_rows, low, high, above, below, pieces, wide, carried, held, surface, columns, cells,
    sensed, right, block, across, layers, gram, stack, made, added,
    load_sem, small_sem, halo_send, halo_recv, m1_send, m1_recv, m2_send, m2_recv,
    send_a, recv_a, send_b, recv_b, send_c, recv_c, send_d, recv_d, send_e, recv_e, send_f, recv_f, own_sem,
):
    c = lax.axis_index("cols")
    s = lax.axis_index("space")
    down, up = lax.rem(s + 1, NS), lax.rem(s + NS - 1, NS)
    y, zh, x = s // 8, lax.rem(s // 4, 2), lax.rem(s, 4)
    plane = y * 4 + x
    others = [lax.rem(c + i, NC) for i in range(1, NC)]
    planes = [lax.rem(plane + i, 16) for i in range(1, 16)]
    space_of = lambda p: (p // 4) * 8 + zh * 4 + lax.rem(p, 4)
    far = y * 8 + (1 - zh) * 4 + x
    line = [(o, s, zh * NC + o) for o in others] + [(o, far, (1 - zh) * NC + o) for o in [c] + others]

    peers = [peer(c, down), peer(c, up)] + [peer(o, t) for o, t, _ in line] + [peer(c, space_of(p)) for p in planes]
    barrier = pltpu.get_barrier_semaphore()
    for device in peers:
        pl.semaphore_signal(barrier, inc=1, device_id=device, device_id_type=MESH)

    def load(i):
        at = pl.ds(pl.multiple_of(i * PER, PER), PER)
        return pltpu.make_async_copy(cov_ref.at[at], cov.at[at], load_sem.at[i])

    def start_load(i, carry):
        load(i).start()
        return carry

    lax.fori_loop(0, CHUNKS, start_load, 0)
    top_row = pl.multiple_of(jnp.maximum(s * TILE - HALO, 0), HALO)
    end_row = pl.multiple_of(jnp.minimum(s * TILE + TILE, NS * TILE - HALO), HALO)
    own_row = pl.multiple_of(s * TILE, TILE)
    smalls = [
        pltpu.make_async_copy(land_ref.at[pl.ds(top_row, HALO)], wet_rows.at[pl.ds(0, HALO)], small_sem.at[0]),
        pltpu.make_async_copy(land_ref.at[pl.ds(own_row, TILE)], wet_rows.at[pl.ds(HALO, TILE)], small_sem.at[1]),
        pltpu.make_async_copy(
            land_ref.at[pl.ds(end_row, HALO)], wet_rows.at[pl.ds(HALO + TILE, HALO)], small_sem.at[2]
        ),
    ]
    for copy in smalls:
        copy.start()
    pieces[1, c] = piece_ref[...]

    def convert(i):
        for n in range(PER):
            k = i * PER + n
            rows = pl.ds(n * 6 * HALO, 6 * HALO)
            upper = [cov[k, pl.ds(TILE * f, HALO)] for f in range(6)]
            lower = [cov[k, pl.ds(TILE * f + HALO, HALO)] for f in range(6)]
            low[i, rows] = jnp.concatenate(upper, axis=0).astype(jnp.bfloat16)
            high[i, rows] = jnp.concatenate(lower, axis=0).astype(jnp.bfloat16)

    def to_down(i):
        return remote(high.at[i], above.at[i], halo_send.at[0, i], halo_recv.at[0, i], peer(c, down))

    def to_up(i):
        return remote(low.at[i], below.at[i], halo_send.at[1, i], halo_recv.at[1, i], peer(c, up))

    load(0).wait()
    convert(0)
    pl.semaphore_wait(barrier, len(peers))
    phase = [
        remote(piece_ref, pieces.at[0, c], m1_send.at[0], m1_recv.at[0], peer(c, down)),
        remote(piece_ref, pieces.at[2, c], m1_send.at[1], m1_recv.at[1], peer(c, up)),
    ]
    for copy in phase:
        copy.start()
    to_down(0).start()
    to_up(0).start()

    def send_halo(i, carry):
        load(i).wait()
        convert(i)
        to_down(i).start()
        to_up(i).start()
        return carry

    lax.fori_loop(1, CHUNKS, send_halo, 0)
    for copy in phase:
        copy.wait()
    shared = []
    for i, o in enumerate(others):
        copy = remote(pieces.at[:, c], pieces.at[:, c], m2_send.at[i], m2_recv.at[c], peer(o, s))
        copy.start()
        shared.append(copy)

    lane = lax.broadcasted_iota(jnp.int32, (WIN, WIDTH), 1)
    first, last = lane == 0, lane == WIDTH - 1
    grid_row = s * TILE - HALO + lax.broadcasted_iota(jnp.int32, (WIN, WIDTH), 0)
    inside = ((grid_row >= 0) & (grid_row < NS * TILE)).astype(jnp.float32)
    for copy in smalls:
        copy.wait()
    wet = wet_rows[...].astype(jnp.float32) * inside
    for o in others:
        remote(pieces.at[:, o], pieces.at[:, o], m2_send.at[0], m2_recv.at[o], peer(o, s)).wait_recv()
    quarter = lax.broadcasted_iota(jnp.int32, (24, 128), 1) // 32
    for slot in range(3):
        for half in range(2):
            for q in range(4):
                rows = jnp.zeros((24, 128), jnp.float32)
                for p in range(4):
                    value = pieces[slot, 4 * half + p]
                    value = pltpu.roll(value, (32 * (p - q)) % 128, 1) if p != q else value
                    rows = jnp.where(quarter == p, value, rows)
                wide[slot, pl.ds(24 * q, 24), 128 * half : 128 * (half + 1)] = rows
    fields = []
    for f in range(6):
        rows = [
            wide[0, pl.ds(TILE * f + HALO, HALO)],
            wide[1, pl.ds(TILE * f, TILE)],
            wide[2, pl.ds(TILE * f, HALO)],
        ]
        fields.append(jnp.concatenate(rows, axis=0) * inside)
    for step in range(STEPS):
        pairs = new_velocities(fields, wet, first, last)
        after = []
        for layer in range(2):
            h = fields[3 * layer]
            depth = (1.0, 2.0)[layer] + h
            u, v = pairs[layer]
            base = 6 * step + 3 * layer
            carried[base] = depth
            carried[base + 1] = u
            carried[base + 2] = v
            h_new = inside * (h - 0.25 * (row_difference(depth * u) + col_difference(depth * v, first, last)))
            after += [h_new, u, v]
        fields = after
    for f in range(6):
        meanf_ref[pl.ds(TILE * f, TILE)] = fields[f][HALO : HALO + TILE]
    surface[pl.ds(NCOL * TILE, TILE)] = (fields[0] + fields[3])[HALO : HALO + TILE]

    def advance(i, carry):
        to_down(i).wait_recv()
        to_up(i).wait_recv()
        for n in range(PER):
            k = i * PER + n
            rows = pl.ds(n * 6 * HALO, 6 * HALO)
            before = above[i, rows].astype(jnp.float32)
            behind = below[i, rows].astype(jnp.float32)
            fields = []
            for f in range(6):
                parts = [
                    before[HALO * f : HALO * (f + 1)],
                    cov[k, pl.ds(TILE * f, TILE)],
                    behind[HALO * f : HALO * (f + 1)],
                ]
                fields.append(jnp.concatenate(parts, axis=0) * inside)
            for step in range(STEPS):
                pairs = new_velocities(fields, wet, first, last)
                after = []
                for layer in range(2):
                    h = fields[3 * layer]
                    u, v = pairs[layer]
                    base = 6 * step + 3 * layer
                    depth = carried[base]
                    rows_flux = depth * u + h * carried[base + 1]
                    cols_flux = depth * v + h * carried[base + 2]
                    change = row_difference(rows_flux) + col_difference(cols_flux, first, last)
                    after += [inside * (h - 0.25 * change), u, v]
                fields = after
            for f in range(6):
                at = pl.ds(pl.multiple_of(k * FR + TILE * f, TILE), TILE)
                for half in range(2):
                    held[half, at] = fields[f][HALO : HALO + TILE, 128 * half : 128 * (half + 1)]
            surface[pl.ds(pl.multiple_of(k * TILE, TILE), TILE)] = (fields[0] + fields[3])[HALO : HALO + TILE]
        return carry

    lax.fori_loop(0, CHUNKS, advance, 0)

    cell = stations_ref[...] - s * (TILE * WIDTH)
    pick = (lax.broadcasted_iota(jnp.int32, (WIDTH, OBS), 0) == cell % WIDTH).astype(jnp.float32)
    at_rows = lax.broadcasted_iota(jnp.int32, (TILE, OBS), 0) == cell // WIDTH
    picked = jnp.dot(surface[...], pick, precision=HIGH, preferred_element_type=jnp.float32)
    picked = picked.reshape(NCOL + 1, TILE, OBS)
    values = jnp.sum(jnp.where(at_rows[None], picked, 0.0), axis=1)
    weight = weight_ref[...]
    mine = values[:NCOL] * weight
    innovation = weight * (observed_ref[...] - values[NCOL:])
    below_first = lax.broadcasted_iota(jnp.int32, (8, OBS), 0) > 0
    sensed[pl.ds(0, NCOL)] = mine
    sensed[pl.ds(NCOL, 8)] = jnp.where(below_first, 0.0, jnp.broadcast_to(innovation, (8, OBS)))
    own_rows = pl.ds(pl.multiple_of(c * NCOL, NCOL), NCOL)
    rows_of = lambda o: pl.ds(pl.multiple_of(o * NCOL, NCOL), NCOL)
    sent = []
    for i, o in enumerate(others):
        copy = remote(sensed.at[pl.ds(0, NCOL)], right.at[own_rows], send_a.at[i], recv_a.at[c], peer(o, s))
        copy.start()
        sent.append(copy)
    right[own_rows] = mine

    def gather_row(fr, carry):
        for half in range(2):
            value = held[half, pl.ds(fr, NCOL, stride=FR)]
            columns[fr, :, 128 * half : 128 * (half + 1)] = value.astype(jnp.bfloat16)
        return carry

    lax.fori_loop(0, FR, gather_row, 0, unroll=8)
    for i, o in enumerate(others):
        source = columns.at[pl.ds(o * PIECE, PIECE)]
        copy = remote(source, cells.at[:, own_rows], send_d.at[i], recv_d.at[c], peer(o, s))
        copy.start()
        sent.append(copy)
    own_cells = pltpu.make_async_copy(columns.at[pl.ds(c * PIECE, PIECE)], cells.at[:, own_rows], own_sem.at[0])
    own_cells.start()

    for o in others:
        source = sensed.at[pl.ds(0, NCOL)]
        remote(source, right.at[rows_of(o)], send_a.at[0], recv_a.at[o], peer(o, s)).wait_recv()
    part = lax.dot_general(
        sensed[...], right[...], (((1,), (1,)), ((), ())), precision=HIGH, preferred_element_type=jnp.float32
    )
    block[...] = part
    for i, p in enumerate(planes):
        copy = remote(block, across.at[plane], send_b.at[i], recv_b.at[plane], peer(c, space_of(p)))
        copy.start()
        sent.append(copy)
    across[plane] = part
    for p in planes:
        remote(block, across.at[p], send_b.at[0], recv_b.at[p], peer(c, space_of(p))).wait_recv()
    total = across[0]
    for p in range(1, 16):
        total = total + across[p]
    place_ = zh * NC + c
    layers[place_] = total
    for i, (o, t, _) in enumerate(line):
        copy = remote(layers.at[place_], layers.at[place_], send_c.at[i], recv_c.at[place_], peer(o, t))
        copy.start()
        sent.append(copy)
    for o, t, slot in line:
        remote(layers.at[slot], layers.at[slot], send_c.at[0], recv_c.at[slot], peer(o, t)).wait_recv()
    for o in range(NC):
        gram[pl.ds(o * NCOL, NCOL)] = layers[o, pl.ds(0, NCOL)] + layers[NC + o, pl.ds(0, NCOL)]
    target = layers[0, pl.ds(NCOL, 8)][:1] + layers[NC, pl.ds(NCOL, 8)][:1]
    factor(gram, stack)
    inverse = stack[:, KALL:]
    halfway = jnp.sum(inverse * target, axis=1, keepdims=True)
    weights = jnp.sum(halfway * inverse, axis=0, keepdims=True)
    w_hi = weights.astype(jnp.bfloat16).astype(jnp.float32)
    w_mid = (weights - w_hi).astype(jnp.bfloat16).astype(jnp.float32)
    w_low = weights - w_hi - w_mid
    row16 = lax.broadcasted_iota(jnp.int32, (NCOL, KALL), 0)
    extra = jnp.where(row16 == 0, w_hi, jnp.where(row16 == 1, w_mid, jnp.where(row16 == 2, w_low, 0.0)))
    transform = jnp.concatenate([inverse.astype(jnp.bfloat16), extra.astype(jnp.bfloat16)], axis=0)

    for o in others:
        source = columns.at[pl.ds(0, PIECE)]
        remote(source, cells.at[:, rows_of(o)], send_d.at[0], recv_d.at[o], peer(o, s)).wait_recv()
    own_cells.wait()
    for g in range(GROUPS):
        for fr in range(g * GROUP, (g + 1) * GROUP):
            out = jnp.dot(transform, cells[fr], preferred_element_type=jnp.float32)
            made[fr] = out[:KALL].astype(jnp.bfloat16)
            added[pl.ds(fr, 1)] = out[KALL : KALL + 1] + out[KALL + 1 : KALL + 2] + out[KALL + 2 : KALL + 3]
        some = pl.ds(g * GROUP, GROUP)
        goal = pl.ds(c * PIECE + g * GROUP, GROUP)
        for i, o in enumerate(others):
            copy = remote(
                made.at[some, rows_of(o)], result_ref.at[goal], send_e.at[g, i], recv_e.at[g, c], peer(o, s)
            )
            copy.start()
            sent.append(copy)
    for i, o in enumerate(others):
        copy = remote(added, increment_ref.at[c], send_f.at[i], recv_f.at[c], peer(o, s))
        copy.start()
        sent.append(copy)
    own_made = pltpu.make_async_copy(
        made.at[:, own_rows], result_ref.at[pl.ds(c * PIECE, PIECE)], own_sem.at[0]
    )
    own_made.start()
    increment_ref[c] = added[...]
    for o in others:
        for g in range(GROUPS):
            theirs = result_ref.at[pl.ds(o * PIECE + g * GROUP, GROUP)]
            some = pl.ds(g * GROUP, GROUP)
            remote(made.at[some, own_rows], theirs, send_e.at[0, 0], recv_e.at[g, o], peer(o, s)).wait_recv()
        remote(added, increment_ref.at[o], send_f.at[0], recv_f.at[o], peer(o, s)).wait_recv()
    own_made.wait()
    for copy in sent + shared:
        copy.wait_send()

    def wait_halo(i, carry):
        to_down(i).wait_send()
        to_up(i).wait_send()
        return carry

    lax.fori_loop(0, CHUNKS, wait_halo, 0)


def filter_step(cov, piece, land, stations, observed, weight):
    dma = pltpu.SemaphoreType.DMA
    f32, bf16 = jnp.float32, jnp.bfloat16
    return pl.pallas_call(
        filter_kernel,
        out_shape=(
            jax.ShapeDtypeStruct((FR, NCOL, WIDTH), bf16),
            jax.ShapeDtypeStruct((NC, NCOL, WIDTH), f32),
            jax.ShapeDtypeStruct((FR, WIDTH), f32),
        ),
        in_specs=[ANY, VMEM, ANY, VMEM, VMEM, VMEM],
        out_specs=(VMEM, VMEM, VMEM),
        scratch_shapes=[
            pltpu.VMEM((NCOL, FR, WIDTH), f32),
            pltpu.VMEM((WIN, WIDTH), jnp.int32),
            pltpu.VMEM((CHUNKS, EDGE, WIDTH), bf16),
            pltpu.VMEM((CHUNKS, EDGE, WIDTH), bf16),
            pltpu.VMEM((CHUNKS, EDGE, WIDTH), bf16),
            pltpu.VMEM((CHUNKS, EDGE, WIDTH), bf16),
            pltpu.VMEM((3, NC, 24, 128), f32),
            pltpu.VMEM((3, FR, WIDTH), f32),
            pltpu.VMEM((6 * STEPS, WIN, WIDTH), f32),
            pltpu.VMEM((2, NCOL * FR, 128), f32),
            pltpu.VMEM(((NCOL + 1) * TILE, WIDTH), f32),
            pltpu.VMEM((FR, NCOL, WIDTH), bf16),
            pltpu.VMEM((PIECE, KALL, WIDTH), bf16),
            pltpu.VMEM((NCOL + 8, OBS), f32),
            pltpu.VMEM((KALL, OBS), f32),
            pltpu.VMEM((NCOL + 8, KALL), f32),
            pltpu.VMEM((16, NCOL + 8, KALL), f32),
            pltpu.VMEM((2 * NC, NCOL + 8, KALL), f32),
            pltpu.VMEM((KALL, KALL), f32),
            pltpu.VMEM((KALL, 2 * KALL), f32),
            pltpu.VMEM((PIECE, KALL, WIDTH), bf16),
            pltpu.VMEM((NCOL, WIDTH), f32),
            dma((CHUNKS,)),
            dma((3,)),
            dma((2, CHUNKS)),
            dma((2, CHUNKS)),
            dma((2,)),
            dma((2,)),
            dma((NC - 1,)),
            dma((NC,)),
            dma((NC - 1,)),
            dma((NC,)),
            dma((15,)),
            dma((16,)),
            dma((15,)),
            dma((16,)),
            dma((NC - 1,)),
            dma((NC,)),
            dma((GROUPS, NC - 1)),
            dma((GROUPS, NC)),
            dma((NC - 1,)),
            dma((NC,)),
            dma((1,)),
        ],
        compiler_params=pltpu.CompilerParams(
            collective_id=0, has_side_effects=True, vmem_limit_bytes=48 * 1024 * 1024
        ),
        name="filter_step",
    )(cov, piece, land, stations, observed, weight)


PAIR = 2


def place_kernel(result_ref, increment_ref, meanf_ref, out_ref, mean_ref, held, total):
    j = pl.program_id(0)

    @pl.when(j == 0)
    def _():
        for half in range(2):
            part = result_ref[:, :, 128 * half : 128 * (half + 1)].astype(jnp.float32)
            held[half] = part.reshape(FR * NCOL, 128)
        for o in range(NC):
            rows = pl.ds(o * PIECE, PIECE)
            total[rows] = meanf_ref[rows] + increment_ref[o][:PIECE]
        c = lax.axis_index("cols")
        width = WIDTH // NC
        turned = pltpu.roll(total[...], lax.rem(WIDTH - c * width, WIDTH), 1)
        mean_ref[...] = turned[:, :width]

    for n in range(PAIR):
        for half in range(2):
            out_ref[n, :, 128 * half : 128 * (half + 1)] = held[half, pl.ds(j * PAIR + n, FR, stride=NCOL)]


def place(result, increment, mean_forecast):
    whole = lambda shape: pl.BlockSpec(shape, lambda i: (0,) * len(shape))
    return pl.pallas_call(
        place_kernel,
        grid=(NCOL // PAIR,),
        out_shape=(
            jax.ShapeDtypeStruct((NCOL, FR, WIDTH), jnp.float32),
            jax.ShapeDtypeStruct((FR, WIDTH // NC), jnp.float32),
        ),
        in_specs=[whole((FR, NCOL, WIDTH)), whole((NC, NCOL, WIDTH)), whole((FR, WIDTH))],
        out_specs=(pl.BlockSpec((PAIR, FR, WIDTH), lambda i: (i, 0, 0)), whole((FR, WIDTH // NC))),
        scratch_shapes=[pltpu.VMEM((2, FR * NCOL, 128), jnp.float32), pltpu.VMEM((FR, WIDTH), jnp.float32)],
        compiler_params=pltpu.CompilerParams(vmem_limit_bytes=24 * 1024 * 1024),
        name="place",
    )(result, increment, mean_forecast)


def local(mean_state, covariance, land_mask, stations, observed, obs_weight):
    piece = mean_state.reshape(4, 24, WIDTH // NC).transpose(1, 0, 2).reshape(24, 128)
    result, increment, mean_forecast = filter_step(
        covariance.reshape(NCOL, FR, WIDTH), piece, land_mask, stations[None], observed[None], obs_weight[None]
    )
    updated, mean = place(result, increment, mean_forecast)
    return mean.reshape(mean_state.shape), updated.reshape(covariance.shape)


def solution(mesh):
    return jax.shard_map(
        local,
        mesh=mesh,
        in_specs=(
            P(None, "space", "cols"),
            P("cols", None, "space", None),
            P(),
            P("space"),
            P("space"),
            P("space"),
        ),
        out_specs=(P(None, "space", "cols"), P("cols", None, "space", None)),
        check_vma=False,
    )
```

time: 874 us -> 108 us (0.12)
  waiting for transfers between devices: 457 us -> 0 us
  blocking collectives: 218 us -> 0 us
  Pallas kernels: 0 us -> 99.7 us
  starting transfers between devices: 99.6 us -> 0 us
  other arithmetic: 46.8 us -> 0 us
  local copies, waits for them, and re-layouts: 27.1 us -> 5.31 us
  between operations: 15.1 us -> 0.65 us
    psum x2 -> x0, waiting for transfers between devices: 366 us -> none  [the longest x1 294 us: local(): gram_sum, target = lax.psum((products, target_part), 'space')]
    psum x1 -> x0, blocking collectives: 113 us -> none  [local(): gram_sum, target = lax.psum((products, target_part), 'space')]
    all_gather x6 -> x0, blocking collectives: 105 us -> none  [the longest x4 73.4 us: local(): carried = lax.all_gather(carried, 'cols', axis=2, tiled=True)]
    pallas_call x0 -> x2, Pallas kernels: none -> 99.7 us  [the longest x1 96.4 us: filter_step(): pl.pallas_call(filter_kernel, out_shape=(jax.ShapeDtypeStruct((FR, NCOL,...]
    ppermute x24 -> x0, starting transfers between devices: 99.5 us -> none  [the longest x12 77.8 us: padded_2(): lax.ppermute(lax.slice_in_dim(block, block.shape[dim] - width, None, axis...]
    all_gather x1 -> x0, waiting for transfers between devices: 77.7 us -> none  [local(): shard_piece = lax.all_gather(columns_low, 'cols', axis=0, tiled=True)]
    another operation x5 -> x0, other arithmetic: 22.9 us -> none  [the longest x3 12.4 us: local(): lower_factor = lax.linalg.cholesky(gram_matrix)]
    ppermute x24 -> x0, waiting for transfers between devices: 13.3 us -> none  [the longest x12 7.28 us: padded_2(): lax.ppermute(lax.slice_in_dim(block, 0, width, axis=dim), axis, backward)]
  transfers between devices with their start and end apart: 27 -> 0, of which waited for: 15 -> 0; matrix products, arithmetic and copies ran while one was open for 2% -> 0% of each run, Pallas kernels for 0% -> 0%
where the time goes in v2:
time: 108 us; the launch traced here: 106 us
  Pallas kernels  99.7 us (92%)
  local copies, waits for them, and re-layouts  5.31 us (5%)
    pallas_call x1, Pallas kernels, filter_step(): pl.pallas_call(filter_kernel, out_shape=(jax.ShapeDtypeStruct((FR, NCOL,...  96.4 us
    unnamed x10, local copies, waits for them, and re-layouts  4.41 us
    pallas_call x1, Pallas kernels, place(): pl.pallas_call(place_kernel, grid=(NCOL // PAIR,), out_shape=(jax.ShapeDt...  3.34 us

profile of v2, /device:TPU:33, one launch (start us, length us, event | category | flops | bytes accessed | tf_op | source)
XLA Modules:
  0.0 105.7 jit_solution(1881758380229256173)
XLA Ops:
  0.6 0.8 copy.10
  1.4 0.1 reshape.21.piece_ref
  1.5 0.0 copy-start
  1.5 1.4 %copy-done = f32[16,6,16,256]{3,2,1,0:T(8,128)S(1)} copy-done((f32[16,6,16,256]{3,2,1,0:T(8,128)S(1)}, f32[16,6,16,256]{3,2,1,0:T(8,128)}, u32[]{:S(2)}) %copy-start) | copy-done | bytes 1572888
  2.9 0.0 copy-start.1
  2.9 1.0 copy-done.1
  4.0 0.0 copy-start.2
  4.0 0.7 copy-done.2
  4.6 0.0 copy-start.3
  4.6 0.7 copy-done.3
  5.3 0.0 copy-start.4
  5.3 0.7 copy-done.4
  6.0 96.4 %filter_step.1 = (bf16[96,16,256]{2,1,0:T(8,128)(2,1)S(1)}, f32[8,16,256]{2,1,0:T(8,128)S(1)}, f32[96,256]{1,0:T(8,128)S(1)}) custom-call(f32[16,96,256]{2,1,0:T(8,128)S(1)} %bitcast.10, f32[24,128]{1,0:T(8,128)S(1)} %reshape.21.piece_ref, s32[512,256]{1,0:T(8,128)S(1)} %copy-done.1, s32[1,128]{1,0:T(1,128)S(1)} %bitcast.11, f32[1,128]{1,0:T(1,128)S(1)} %bitcast.12, ...), custom_call_target="tpu_custom_call" | custom-call | tf_op jit(solution)/shard_map/filter_step/pallas_call | solution.py:409
  102.3 3.3 %place.1 = (f32[16,96,256]{2,1,0:T(8,128)}, f32[96,32]{1,0:T(8,128)}) custom-call(bf16[96,16,256]{2,1,0:T(8,128)(2,1)S(1)} %get-tuple-element.7.result_ref, f32[8,16,256]{2,1,0:T(8,128)S(1)} %get-tuple-element.8.increment_ref, f32[96,256]{1,0:T(8,128)S(1)} %get-tuple-element.9.meanf_ref), custom_call_target="tpu_custom_call" | custom-call | tf_op jit(solution)/shard_map/place/pallas_call | solution.py:496
Async XLA Ops:
  1.5 1.4 %copy-start = (f32[16,6,16,256]{3,2,1,0:T(8,128)S(1)}, f32[16,6,16,256]{3,2,1,0:T(8,128)}, u32[]{:S(2)}) copy-start(f32[16,6,16,256]{3,2,1,0:T(8,128)} %param.7) | copy-start | bytes 4718596
  2.9 1.0 copy-start.1
  4.0 0.7 copy-start.2
  4.6 0.7 copy-start.3
  5.3 0.7 copy-start.4

commit v3 on v2

--- a/solution.py
+++ b/solution.py
@@ -22,6 +22,7 @@
 MESH = pl.DeviceIdType.MESH
 ANY = pl.BlockSpec(memory_space=pl.ANY)
 VMEM = pl.BlockSpec(memory_space=pltpu.VMEM)
+HBM = pl.BlockSpec(memory_space=pltpu.HBM)
 
 
 def peer(c, s):
@@ -105,6 +106,7 @@
 
 
 CHUNKS = 8
+AHEAD = 4
 PER = NCOL // CHUNKS
 EDGE = PER * 6 * HALO
 GROUPS = 4
@@ -112,9 +114,9 @@
 
 
 def filter_kernel(
-    cov_ref, piece_ref, land_ref, stations_ref, observed_ref, weight_ref,
+    cov_ref, piece_ref, land_ref, stations_hbm, observed_hbm, weight_hbm,
     result_ref, increment_ref, meanf_ref,
-    cov, wet_rows, low, high, above, below, pieces, wide, carried, held, surface, columns, cells,
+    cov, wet_rows, stations_ref, observed_ref, weight_ref, low, high, above, below, pieces, wide, carried, held, surface, columns, cells,
     sensed, right, block, across, layers, gram, stack, made, added,
     load_sem, small_sem, halo_send, halo_recv, m1_send, m1_recv, m2_send, m2_recv,
     send_a, recv_a, send_b, recv_b, send_c, recv_c, send_d, recv_d, send_e, recv_e, send_f, recv_f, own_sem,
@@ -128,9 +130,14 @@
     planes = [lax.rem(plane + i, 16) for i in range(1, 16)]
     space_of = lambda p: (p // 4) * 8 + zh * 4 + lax.rem(p, 4)
     far = y * 8 + (1 - zh) * 4 + x
-    line = [(o, s, zh * NC + o) for o in others] + [(o, far, (1 - zh) * NC + o) for o in [c] + others]
-
-    peers = [peer(c, down), peer(c, up)] + [peer(o, t) for o, t, _ in line] + [peer(c, space_of(p)) for p in planes]
+    chip, core = c // 2, lax.rem(c, 2)
+    partner = 2 * chip + 1 - core
+    chips = [lax.rem(chip + i, 4) for i in range(1, 4)]
+    line = [(q, s, zh) for q in chips] + [(q, far, 1 - zh) for q in [chip] + chips]
+    same_core = lambda q: 2 * q + core
+
+    peers = [peer(c, down), peer(c, up)] + [peer(o, s) for o in others]
+    peers += [peer(same_core(q), far) for q in [chip] + chips] + [peer(c, space_of(p)) for p in planes]
     barrier = pltpu.get_barrier_semaphore()
     for device in peers:
         pl.semaphore_signal(barrier, inc=1, device_id=device, device_id_type=MESH)
@@ -153,10 +160,14 @@
         pltpu.make_async_copy(
             land_ref.at[pl.ds(end_row, HALO)], wet_rows.at[pl.ds(HALO + TILE, HALO)], small_sem.at[2]
         ),
+        pltpu.make_async_copy(stations_hbm, stations_ref, small_sem.at[3]),
+        pltpu.make_async_copy(observed_hbm, observed_ref, small_sem.at[4]),
+        pltpu.make_async_copy(weight_hbm, weight_ref, small_sem.at[5]),
     ]
     for copy in smalls:
         copy.start()
-    pieces[1, c] = piece_ref[...]
+    pieces[core, chip, 1] = piece_ref[0]
+    pieces[core, chip, 2] = piece_ref[1]
 
     def convert(i):
         for n in range(PER):
@@ -177,8 +188,8 @@
     convert(0)
     pl.semaphore_wait(barrier, len(peers))
     phase = [
-        remote(piece_ref, pieces.at[0, c], m1_send.at[0], m1_recv.at[0], peer(c, down)),
-        remote(piece_ref, pieces.at[2, c], m1_send.at[1], m1_recv.at[1], peer(c, up)),
+        remote(piece_ref.at[1], pieces.at[core, chip, 0], m1_send.at[0], m1_recv.at[0], peer(c, down)),
+        remote(piece_ref.at[0], pieces.at[core, chip, 3], m1_send.at[1], m1_recv.at[1], peer(c, up)),
     ]
     for copy in phase:
         copy.start()
@@ -188,16 +199,21 @@
     def send_halo(i, carry):
         load(i).wait()
         convert(i)
-        to_down(i).start()
-        to_up(i).start()
+
+        @pl.when(i < AHEAD)
+        def _():
+            to_down(i).start()
+            to_up(i).start()
+
         return carry
 
     lax.fori_loop(1, CHUNKS, send_halo, 0)
     for copy in phase:
         copy.wait()
     shared = []
-    for i, o in enumerate(others):
-        copy = remote(pieces.at[:, c], pieces.at[:, c], m2_send.at[i], m2_recv.at[c], peer(o, s))
+    for i, q in enumerate(chips):
+        ours = pieces.at[core, chip]
+        copy = remote(ours, ours, m2_send.at[i], m2_recv.at[chip], peer(same_core(q), s))
         copy.start()
         shared.append(copy)
 
@@ -208,25 +224,25 @@
     for copy in smalls:
         copy.wait()
     wet = wet_rows[...].astype(jnp.float32) * inside
-    for o in others:
-        remote(pieces.at[:, o], pieces.at[:, o], m2_send.at[0], m2_recv.at[o], peer(o, s)).wait_recv()
-    quarter = lax.broadcasted_iota(jnp.int32, (24, 128), 1) // 32
-    for slot in range(3):
+    for q in chips:
+        theirs = pieces.at[core, q]
+        remote(theirs, theirs, m2_send.at[0], m2_recv.at[q], peer(same_core(q), s)).wait_recv()
+    swap = remote(pieces.at[core], pieces.at[core], m2_send.at[3], m2_recv.at[4], peer(partner, s))
+    swap.start()
+    swap.wait()
+    quarter = lax.broadcasted_iota(jnp.int32, (12, 128), 1) // 32
+    for slot in range(4):
         for half in range(2):
             for q in range(4):
-                rows = jnp.zeros((24, 128), jnp.float32)
+                rows = jnp.zeros((12, 128), jnp.float32)
                 for p in range(4):
-                    value = pieces[slot, 4 * half + p]
+                    value = pieces[p % 2, 2 * half + p // 2, slot]
                     value = pltpu.roll(value, (32 * (p - q)) % 128, 1) if p != q else value
                     rows = jnp.where(quarter == p, value, rows)
-                wide[slot, pl.ds(24 * q, 24), 128 * half : 128 * (half + 1)] = rows
+                wide[slot, pl.ds(12 * q, 12), 128 * half : 128 * (half + 1)] = rows
     fields = []
     for f in range(6):
-        rows = [
-            wide[0, pl.ds(TILE * f + HALO, HALO)],
-            wide[1, pl.ds(TILE * f, TILE)],
-            wide[2, pl.ds(TILE * f, HALO)],
-        ]
+        rows = [wide[slot, pl.ds(HALO * f, HALO)] for slot in range(4)]
         fields.append(jnp.concatenate(rows, axis=0) * inside)
     for step in range(STEPS):
         pairs = new_velocities(fields, wet, first, last)
@@ -247,6 +263,14 @@
     surface[pl.ds(NCOL * TILE, TILE)] = (fields[0] + fields[3])[HALO : HALO + TILE]
 
     def advance(i, carry):
+        to_down(i).wait_send()
+        to_up(i).wait_send()
+
+        @pl.when(i + AHEAD < CHUNKS)
+        def _():
+            to_down(i + AHEAD).start()
+            to_up(i + AHEAD).start()
+
         to_down(i).wait_recv()
         to_up(i).wait_recv()
         for n in range(PER):
@@ -299,11 +323,12 @@
     own_rows = pl.ds(pl.multiple_of(c * NCOL, NCOL), NCOL)
     rows_of = lambda o: pl.ds(pl.multiple_of(o * NCOL, NCOL), NCOL)
     sent = []
-    for i, o in enumerate(others):
-        copy = remote(sensed.at[pl.ds(0, NCOL)], right.at[own_rows], send_a.at[i], recv_a.at[c], peer(o, s))
+    for i, q in enumerate(chips):
+        source = sensed.at[pl.ds(0, NCOL)]
+        copy = remote(source, right.at[chip, core], send_a.at[i], recv_a.at[chip], peer(same_core(q), s))
         copy.start()
         sent.append(copy)
-    right[own_rows] = mine
+    right[chip, core] = mine
 
     def gather_row(fr, carry):
         for half in range(2):
@@ -320,11 +345,18 @@
     own_cells = pltpu.make_async_copy(columns.at[pl.ds(c * PIECE, PIECE)], cells.at[:, own_rows], own_sem.at[0])
     own_cells.start()
 
-    for o in others:
+    for q in chips:
         source = sensed.at[pl.ds(0, NCOL)]
-        remote(source, right.at[rows_of(o)], send_a.at[0], recv_a.at[o], peer(o, s)).wait_recv()
+        remote(source, right.at[q, core], send_a.at[0], recv_a.at[q], peer(same_core(q), s)).wait_recv()
+    swap = remote(right.at[:, core], right.at[:, core], send_a.at[3], recv_a.at[4], peer(partner, s))
+    swap.start()
+    swap.wait()
     part = lax.dot_general(
-        sensed[...], right[...], (((1,), (1,)), ((), ())), precision=HIGH, preferred_element_type=jnp.float32
+        sensed[...],
+        right[...].reshape(KALL, OBS),
+        (((1,), (1,)), ((), ())),
+        precision=HIGH,
+        preferred_element_type=jnp.float32,
     )
     block[...] = part
     for i, p in enumerate(planes):
@@ -337,17 +369,22 @@
     total = across[0]
     for p in range(1, 16):
         total = total + across[p]
-    place_ = zh * NC + c
-    layers[place_] = total
-    for i, (o, t, _) in enumerate(line):
-        copy = remote(layers.at[place_], layers.at[place_], send_c.at[i], recv_c.at[place_], peer(o, t))
+    layers[core, zh, chip] = total
+    for i, (q, t, _) in enumerate(line):
+        ours = layers.at[core, zh, chip]
+        copy = remote(ours, ours, send_c.at[i], recv_c.at[zh, chip], peer(same_core(q), t))
         copy.start()
         sent.append(copy)
-    for o, t, slot in line:
-        remote(layers.at[slot], layers.at[slot], send_c.at[0], recv_c.at[slot], peer(o, t)).wait_recv()
+    for q, t, side in line:
+        theirs = layers.at[core, side, q]
+        remote(theirs, theirs, send_c.at[0], recv_c.at[side, q], peer(same_core(q), t)).wait_recv()
+    swap = remote(layers.at[core], layers.at[core], send_c.at[7], recv_c.at[2, 0], peer(partner, s))
+    swap.start()
+    swap.wait()
     for o in range(NC):
-        gram[pl.ds(o * NCOL, NCOL)] = layers[o, pl.ds(0, NCOL)] + layers[NC + o, pl.ds(0, NCOL)]
-    target = layers[0, pl.ds(NCOL, 8)][:1] + layers[NC, pl.ds(NCOL, 8)][:1]
+        both = [layers[o % 2, side, o // 2, pl.ds(0, NCOL)] for side in range(2)]
+        gram[pl.ds(o * NCOL, NCOL)] = both[0] + both[1]
+    target = layers[0, 0, 0, pl.ds(NCOL, 8)][:1] + layers[0, 1, 0, pl.ds(NCOL, 8)][:1]
     factor(gram, stack)
     inverse = stack[:, KALL:]
     halfway = jnp.sum(inverse * target, axis=1, keepdims=True)
@@ -395,13 +432,6 @@
     for copy in sent + shared:
         copy.wait_send()
 
-    def wait_halo(i, carry):
-        to_down(i).wait_send()
-        to_up(i).wait_send()
-        return carry
-
-    lax.fori_loop(0, CHUNKS, wait_halo, 0)
-
 
 def filter_step(cov, piece, land, stations, observed, weight):
     dma = pltpu.SemaphoreType.DMA
@@ -413,45 +443,48 @@
             jax.ShapeDtypeStruct((NC, NCOL, WIDTH), f32),
             jax.ShapeDtypeStruct((FR, WIDTH), f32),
         ),
-        in_specs=[ANY, VMEM, ANY, VMEM, VMEM, VMEM],
+        in_specs=[HBM, VMEM, HBM, HBM, HBM, HBM],
         out_specs=(VMEM, VMEM, VMEM),
         scratch_shapes=[
             pltpu.VMEM((NCOL, FR, WIDTH), f32),
             pltpu.VMEM((WIN, WIDTH), jnp.int32),
+            pltpu.VMEM((1, OBS), jnp.int32),
+            pltpu.VMEM((1, OBS), f32),
+            pltpu.VMEM((1, OBS), f32),
             pltpu.VMEM((CHUNKS, EDGE, WIDTH), bf16),
             pltpu.VMEM((CHUNKS, EDGE, WIDTH), bf16),
             pltpu.VMEM((CHUNKS, EDGE, WIDTH), bf16),
             pltpu.VMEM((CHUNKS, EDGE, WIDTH), bf16),
-            pltpu.VMEM((3, NC, 24, 128), f32),
-            pltpu.VMEM((3, FR, WIDTH), f32),
+            pltpu.VMEM((2, 4, 4, 12, 128), f32),
+            pltpu.VMEM((4, 6 * HALO, WIDTH), f32),
             pltpu.VMEM((6 * STEPS, WIN, WIDTH), f32),
             pltpu.VMEM((2, NCOL * FR, 128), f32),
             pltpu.VMEM(((NCOL + 1) * TILE, WIDTH), f32),
             pltpu.VMEM((FR, NCOL, WIDTH), bf16),
             pltpu.VMEM((PIECE, KALL, WIDTH), bf16),
             pltpu.VMEM((NCOL + 8, OBS), f32),
-            pltpu.VMEM((KALL, OBS), f32),
+            pltpu.VMEM((4, 2, NCOL, OBS), f32),
             pltpu.VMEM((NCOL + 8, KALL), f32),
             pltpu.VMEM((16, NCOL + 8, KALL), f32),
-            pltpu.VMEM((2 * NC, NCOL + 8, KALL), f32),
+            pltpu.VMEM((2, 2, 4, NCOL + 8, KALL), f32),
             pltpu.VMEM((KALL, KALL), f32),
             pltpu.VMEM((KALL, 2 * KALL), f32),
             pltpu.VMEM((PIECE, KALL, WIDTH), bf16),
             pltpu.VMEM((NCOL, WIDTH), f32),
             dma((CHUNKS,)),
-            dma((3,)),
+            dma((6,)),
             dma((2, CHUNKS)),
             dma((2, CHUNKS)),
             dma((2,)),
             dma((2,)),
-            dma((NC - 1,)),
-            dma((NC,)),
-            dma((NC - 1,)),
-            dma((NC,)),
+            dma((4,)),
+            dma((5,)),
+            dma((4,)),
+            dma((5,)),
             dma((15,)),
             dma((16,)),
-            dma((15,)),
-            dma((16,)),
+            dma((8,)),
+            dma((3, 4)),
             dma((NC - 1,)),
             dma((NC,)),
             dma((GROUPS, NC - 1)),
@@ -461,7 +494,7 @@
             dma((1,)),
         ],
         compiler_params=pltpu.CompilerParams(
-            collective_id=0, has_side_effects=True, vmem_limit_bytes=48 * 1024 * 1024
+            collective_id=0, has_side_effects=True, vmem_limit_bytes=60 * 1024 * 1024
         ),
         name="filter_step",
     )(cov, piece, land, stations, observed, weight)
@@ -509,7 +542,9 @@
 
 
 def local(mean_state, covariance, land_mask, stations, observed, obs_weight):
-    piece = mean_state.reshape(4, 24, WIDTH // NC).transpose(1, 0, 2).reshape(24, 128)
+    width = WIDTH // NC
+    halves = mean_state.reshape(6, 2, HALO, width).transpose(1, 0, 2, 3)
+    piece = halves.reshape(2, 4, 12, width).transpose(0, 2, 1, 3).reshape(2, 12, 128)
     result, increment, mean_forecast = filter_step(
         covariance.reshape(NCOL, FR, WIDTH), piece, land_mask, stations[None], observed[None], obs_weight[None]
     )

time: 108 us -> 103 us (0.954)
  Pallas kernels: 99.7 us -> 95.7 us
    pallas_call x1, Pallas kernels: 96.4 us -> 92.4 us  [filter_step(): pl.pallas_call(filter_kernel, out_shape=(jax.ShapeDtypeStruct((FR, NCOL,...]
    unnamed x10 -> x6, local copies, waits for them, and re-layouts: 4.41 us -> 2.92 us
where the time goes in v3:
time: 103 us; the launch traced here: 101 us
  Pallas kernels  95.7 us (93%)
  local copies, waits for them, and re-layouts  4.46 us (4%)
    pallas_call x1, Pallas kernels, filter_step(): pl.pallas_call(filter_kernel, out_shape=(jax.ShapeDtypeStruct((FR, NCOL,...  92.4 us
    pallas_call x1, Pallas kernels, place(): pl.pallas_call(place_kernel, grid=(NCOL // PAIR,), out_shape=(jax.ShapeDt...  3.31 us
    unnamed x6, local copies, waits for them, and re-layouts  2.92 us

profile of v3, /device:TPU:33, one launch (start us, length us, event | category | flops | bytes accessed | tf_op | source)
XLA Modules:
  0.0 100.8 jit_solution(2769526226317618311)
XLA Ops:
  0.6 0.8 copy.8
  1.5 0.7 reshape.28.piece_ref
  2.2 92.4 %filter_step.1 = (bf16[96,16,256]{2,1,0:T(8,128)(2,1)}, f32[8,16,256]{2,1,0:T(8,128)}, f32[96,256]{1,0:T(8,128)}) custom-call(f32[16,96,256]{2,1,0:T(8,128)} %bitcast.12, f32[2,12,128]{2,1,0:T(8,128)} %reshape.28.piece_ref, s32[512,256]{1,0:T(8,128)} %land_ref.1, s32[1,128]{1,0:T(1,128)} %bitcast.15, f32[1,128]{1,0:T(1,128)} %bitcast.16, f32[1,128]{1,0:T(1,128)} %bitcast.17), custom_call_target="tpu_custom_call" | custom-call | tf_op jit(solution)/shard_map/filter_step/pallas_call | solution.py:439
  94.5 0.0 copy-start
  94.6 1.1 %copy-done = bf16[96,16,256]{2,1,0:T(8,128)(2,1)S(1)} copy-done((bf16[96,16,256]{2,1,0:T(8,128)(2,1)S(1)}, bf16[96,16,256]{2,1,0:T(8,128)(2,1)}, u32[]{:S(2)}) %copy-start) | copy-done | bytes 786456
  95.7 0.0 copy-start.1
  95.7 0.9 copy-done.1
  96.6 0.0 copy-start.2
  96.6 0.9 copy-done.2
  97.5 3.3 %place.1 = (f32[16,96,256]{2,1,0:T(8,128)}, f32[96,32]{1,0:T(8,128)}) custom-call(bf16[96,16,256]{2,1,0:T(8,128)(2,1)S(1)} %copy-done, f32[8,16,256]{2,1,0:T(8,128)S(1)} %copy-done.1, f32[96,256]{1,0:T(8,128)S(1)} %copy-done.2), custom_call_target="tpu_custom_call" | custom-call | tf_op jit(solution)/shard_map/place/pallas_call | solution.py:529
  (1 shorter events, 0.0 us)
Async XLA Ops:
  94.5 1.1 %copy-start = (bf16[96,16,256]{2,1,0:T(8,128)(2,1)S(1)}, bf16[96,16,256]{2,1,0:T(8,128)(2,1)}, u32[]{:S(2)}) copy-start(bf16[96,16,256]{2,1,0:T(8,128)(2,1)} %get-tuple-element.7.result_ref) | copy-start | bytes 2359300
  95.7 0.9 copy-start.1
  96.6 0.9 copy-start.2

commit v4 on v3

--- a/solution.py
+++ b/solution.py
@@ -106,7 +106,8 @@
 
 
 CHUNKS = 8
-AHEAD = 4
+FIRST = 4
+ON0, FAR1, ON1 = 0, 1, 4
 PER = NCOL // CHUNKS
 EDGE = PER * 6 * HALO
 GROUPS = 4
@@ -114,11 +115,11 @@
 
 
 def filter_kernel(
-    cov_ref, piece_ref, land_ref, stations_hbm, observed_hbm, weight_hbm,
+    cov_ref, mean_hbm, land_ref, stations_hbm, observed_hbm, weight_hbm,
     result_ref, increment_ref, meanf_ref,
-    cov, wet_rows, stations_ref, observed_ref, weight_ref, low, high, above, below, pieces, wide, carried, held, surface, columns, cells,
+    cov, wet_rows, stations_ref, observed_ref, weight_ref, low, high, above, below, relay, mean_in, mean_rows, piece_ref, pieces, wide, carried, held, surface, columns, cells,
     sensed, right, block, across, layers, gram, stack, made, added,
-    load_sem, small_sem, halo_send, halo_recv, m1_send, m1_recv, m2_send, m2_recv,
+    load_sem, small_sem, halo_send, halo_recv, relay_send, relay_recv, m_send, m_recv,
     send_a, recv_a, send_b, recv_b, send_c, recv_c, send_d, recv_d, send_e, recv_e, send_f, recv_f, own_sem,
 ):
     c = lax.axis_index("cols")
@@ -136,7 +137,7 @@
     line = [(q, s, zh) for q in chips] + [(q, far, 1 - zh) for q in [chip] + chips]
     same_core = lambda q: 2 * q + core
 
-    peers = [peer(c, down), peer(c, up)] + [peer(o, s) for o in others]
+    peers = [peer(same_core(q), t) for t in (down, up) for q in [chip] + chips] + [peer(o, s) for o in others]
     peers += [peer(same_core(q), far) for q in [chip] + chips] + [peer(c, space_of(p)) for p in planes]
     barrier = pltpu.get_barrier_semaphore()
     for device in peers:
@@ -150,7 +151,6 @@
         load(i).start()
         return carry
 
-    lax.fori_loop(0, CHUNKS, start_load, 0)
     top_row = pl.multiple_of(jnp.maximum(s * TILE - HALO, 0), HALO)
     end_row = pl.multiple_of(jnp.minimum(s * TILE + TILE, NS * TILE - HALO), HALO)
     own_row = pl.multiple_of(s * TILE, TILE)
@@ -164,10 +164,18 @@
         pltpu.make_async_copy(observed_hbm, observed_ref, small_sem.at[4]),
         pltpu.make_async_copy(weight_hbm, weight_ref, small_sem.at[5]),
     ]
+    load_mean = pltpu.make_async_copy(mean_hbm, mean_in, small_sem.at[6])
+    load_mean.start()
+    lax.fori_loop(0, CHUNKS, start_load, 0)
     for copy in smalls:
         copy.start()
-    pieces[core, chip, 1] = piece_ref[0]
-    pieces[core, chip, 2] = piece_ref[1]
+    load_mean.wait()
+    for part in range(2):
+        for f in range(6):
+            mean_rows[part, pl.ds(HALO * f, HALO)] = mean_in[f, pl.ds(HALO * part, HALO)]
+        packed = jnp.concatenate([mean_rows[part, pl.ds(12 * q, 12)] for q in range(4)], axis=1)
+        piece_ref[part] = packed
+        pieces[core, chip, 1 + part] = packed
 
     def convert(i):
         for n in range(PER):
@@ -181,41 +189,95 @@
     def to_down(i):
         return remote(high.at[i], above.at[i], halo_send.at[0, i], halo_recv.at[0, i], peer(c, down))
 
+    run = y * 8 + zh * 4
+    between = (x == 1) | (x == 2)
+    next_run = jnp.where(zh == 1, y * 8 + 4, lax.rem(y + 1, 4) * 8)
+    last_run = jnp.where(zh == 0, y * 8 + 3, lax.rem(y + 3, 4) * 8 + 7)
+
+    def start_halo(i):
+        odd = lax.rem(i, 2) == 1
+        slot = i // 4
+        inner = peer(c, run + 1 + lax.rem(i // 2, 2))
+
+        def one(way, end, direct, source):
+            @pl.when(odd & end)
+            def _():
+                at = relay.at[0, way, slot]
+                remote(source.at[i], at, halo_send.at[way, i], relay_recv.at[0, way, slot], inner).start()
+
+            @pl.when(jnp.logical_not(odd & end))
+            def _():
+                direct(i).start()
+
+        one(0, x == 3, to_down, high)
+        one(1, x == 0, to_up, low)
+
+    def relay_far(way, slot):
+        return remote(
+            relay.at[0, way, slot], relay.at[1, way, slot],
+            relay_send.at[0, way, slot], relay_recv.at[1, way, slot], peer(c, far),
+        )
+
+    def relay_on(way, slot):
+        i = 4 * slot + 2 * x - 1
+        goal = (above, below)[way].at[i]
+        device = peer(c, (next_run, last_run)[way])
+        return remote(relay.at[1, way, slot], goal, relay_send.at[1, way, slot], halo_recv.at[way, i], device)
+
+    def pass_far(slot):
+        @pl.when(between)
+        def _():
+            for way in range(2):
+                source = (high, low)[way].at[0]
+                recv = relay_recv.at[0, way, slot]
+                remote(source, relay.at[0, way, slot], halo_send.at[way, 0], recv, peer(c, down)).wait_recv()
+                relay_far(way, slot).start()
+
+    def pass_on(slot):
+        @pl.when(between)
+        def _():
+            for way in range(2):
+                relay_far(way, slot).wait_recv()
+                relay_on(way, slot).start()
+
     def to_up(i):
         return remote(low.at[i], below.at[i], halo_send.at[1, i], halo_recv.at[1, i], peer(c, up))
 
     load(0).wait()
     convert(0)
     pl.semaphore_wait(barrier, len(peers))
-    phase = [
-        remote(piece_ref.at[1], pieces.at[core, chip, 0], m1_send.at[0], m1_recv.at[0], peer(c, down)),
-        remote(piece_ref.at[0], pieces.at[core, chip, 3], m1_send.at[1], m1_recv.at[1], peer(c, up)),
-    ]
-    for copy in phase:
+    shared = []
+    for i, q in enumerate([chip] + chips):
+        device = same_core(q)
+        to = lambda kind: (m_send.at[kind, i], m_recv.at[kind, chip])
+        shared.append(remote(piece_ref.at[1], pieces.at[core, chip, 0], *to(0), peer(device, down)))
+        shared.append(remote(piece_ref.at[0], pieces.at[core, chip, 3], *to(2), peer(device, up)))
+        if i:
+            shared.append(remote(piece_ref, pieces.at[core, chip, pl.ds(1, 2)], *to(1), peer(device, s)))
+    for copy in shared:
         copy.start()
-    to_down(0).start()
-    to_up(0).start()
+    start_halo(0)
 
     def send_halo(i, carry):
         load(i).wait()
         convert(i)
 
-        @pl.when(i < AHEAD)
+        @pl.when(i < FIRST)
         def _():
-            to_down(i).start()
-            to_up(i).start()
+            start_halo(i)
 
         return carry
 
     lax.fori_loop(1, CHUNKS, send_halo, 0)
-    for copy in phase:
-        copy.wait()
-    shared = []
-    for i, q in enumerate(chips):
-        ours = pieces.at[core, chip]
-        copy = remote(ours, ours, m2_send.at[i], m2_recv.at[chip], peer(same_core(q), s))
-        copy.start()
-        shared.append(copy)
+    pass_far(0)
+
+    def send_more(i, carry):
+        to_down(i - FIRST).wait_send()
+        to_up(i - FIRST).wait_send()
+        start_halo(i)
+        return carry
+
+    lax.fori_loop(FIRST, CHUNKS, send_more, 0)
 
     lane = lax.broadcasted_iota(jnp.int32, (WIN, WIDTH), 1)
     first, last = lane == 0, lane == WIDTH - 1
@@ -224,10 +286,14 @@
     for copy in smalls:
         copy.wait()
     wet = wet_rows[...].astype(jnp.float32) * inside
-    for q in chips:
-        theirs = pieces.at[core, q]
-        remote(theirs, theirs, m2_send.at[0], m2_recv.at[q], peer(same_core(q), s)).wait_recv()
-    swap = remote(pieces.at[core], pieces.at[core], m2_send.at[3], m2_recv.at[4], peer(partner, s))
+    for i, q in enumerate([chip] + chips):
+        device = peer(same_core(q), down)
+        remote(piece_ref.at[1], pieces.at[core, q, 0], m_send.at[0, 0], m_recv.at[0, q], device).wait_recv()
+        remote(piece_ref.at[0], pieces.at[core, q, 3], m_send.at[0, 0], m_recv.at[2, q], device).wait_recv()
+        if i:
+            theirs = pieces.at[core, q, pl.ds(1, 2)]
+            remote(piece_ref, theirs, m_send.at[0, 0], m_recv.at[1, q], device).wait_recv()
+    swap = remote(pieces.at[core], pieces.at[core], m_send.at[1, 0], m_recv.at[1, chip], peer(partner, s))
     swap.start()
     swap.wait()
     quarter = lax.broadcasted_iota(jnp.int32, (12, 128), 1) // 32
@@ -263,13 +329,11 @@
     surface[pl.ds(NCOL * TILE, TILE)] = (fields[0] + fields[3])[HALO : HALO + TILE]
 
     def advance(i, carry):
-        to_down(i).wait_send()
-        to_up(i).wait_send()
-
-        @pl.when(i + AHEAD < CHUNKS)
-        def _():
-            to_down(i + AHEAD).start()
-            to_up(i + AHEAD).start()
+        for at, action, slot in ((ON0, pass_on, 0), (FAR1, pass_far, 1), (ON1, pass_on, 1)):
+
+            @pl.when(i == at)
+            def _():
+                action(slot)
 
         to_down(i).wait_recv()
         to_up(i).wait_recv()
@@ -432,8 +496,22 @@
     for copy in sent + shared:
         copy.wait_send()
 
-
-def filter_step(cov, piece, land, stations, observed, weight):
+    def wait_halo(i, carry):
+        to_down(i).wait_send()
+        to_up(i).wait_send()
+        return carry
+
+    lax.fori_loop(CHUNKS - FIRST, CHUNKS, wait_halo, 0)
+
+    @pl.when(between)
+    def _():
+        for way in range(2):
+            for slot in range(2):
+                relay_far(way, slot).wait_send()
+                relay_on(way, slot).wait_send()
+
+
+def filter_step(cov, mean, land, stations, observed, weight):
     dma = pltpu.SemaphoreType.DMA
     f32, bf16 = jnp.float32, jnp.bfloat16
     return pl.pallas_call(
@@ -443,7 +521,7 @@
             jax.ShapeDtypeStruct((NC, NCOL, WIDTH), f32),
             jax.ShapeDtypeStruct((FR, WIDTH), f32),
         ),
-        in_specs=[HBM, VMEM, HBM, HBM, HBM, HBM],
+        in_specs=[HBM] * 6,
         out_specs=(VMEM, VMEM, VMEM),
         scratch_shapes=[
             pltpu.VMEM((NCOL, FR, WIDTH), f32),
@@ -455,6 +533,10 @@
             pltpu.VMEM((CHUNKS, EDGE, WIDTH), bf16),
             pltpu.VMEM((CHUNKS, EDGE, WIDTH), bf16),
             pltpu.VMEM((CHUNKS, EDGE, WIDTH), bf16),
+            pltpu.VMEM((2, 2, 2, EDGE, WIDTH), bf16),
+            pltpu.VMEM((6, TILE, WIDTH // NC), f32),
+            pltpu.VMEM((2, 6 * HALO, WIDTH // NC), f32),
+            pltpu.VMEM((2, 12, 128), f32),
             pltpu.VMEM((2, 4, 4, 12, 128), f32),
             pltpu.VMEM((4, 6 * HALO, WIDTH), f32),
             pltpu.VMEM((6 * STEPS, WIN, WIDTH), f32),
@@ -472,13 +554,13 @@
             pltpu.VMEM((PIECE, KALL, WIDTH), bf16),
             pltpu.VMEM((NCOL, WIDTH), f32),
             dma((CHUNKS,)),
-            dma((6,)),
+            dma((7,)),
             dma((2, CHUNKS)),
             dma((2, CHUNKS)),
-            dma((2,)),
-            dma((2,)),
-            dma((4,)),
-            dma((5,)),
+            dma((2, 2, 2)),
+            dma((2, 2, 2)),
+            dma((3, 4)),
+            dma((3, 4)),
             dma((4,)),
             dma((5,)),
             dma((15,)),
@@ -497,7 +579,7 @@
             collective_id=0, has_side_effects=True, vmem_limit_bytes=60 * 1024 * 1024
         ),
         name="filter_step",
-    )(cov, piece, land, stations, observed, weight)
+    )(cov, mean, land, stations, observed, weight)
 
 
 PAIR = 2
@@ -536,17 +618,14 @@
         in_specs=[whole((FR, NCOL, WIDTH)), whole((NC, NCOL, WIDTH)), whole((FR, WIDTH))],
         out_specs=(pl.BlockSpec((PAIR, FR, WIDTH), lambda i: (i, 0, 0)), whole((FR, WIDTH // NC))),
         scratch_shapes=[pltpu.VMEM((2, FR * NCOL, 128), jnp.float32), pltpu.VMEM((FR, WIDTH), jnp.float32)],
-        compiler_params=pltpu.CompilerParams(vmem_limit_bytes=24 * 1024 * 1024),
+        compiler_params=pltpu.CompilerParams(vmem_limit_bytes=60 * 1024 * 1024),
         name="place",
     )(result, increment, mean_forecast)
 
 
 def local(mean_state, covariance, land_mask, stations, observed, obs_weight):
-    width = WIDTH // NC
-    halves = mean_state.reshape(6, 2, HALO, width).transpose(1, 0, 2, 3)
-    piece = halves.reshape(2, 4, 12, width).transpose(0, 2, 1, 3).reshape(2, 12, 128)
     result, increment, mean_forecast = filter_step(
-        covariance.reshape(NCOL, FR, WIDTH), piece, land_mask, stations[None], observed[None], obs_weight[None]
+        covariance.reshape(NCOL, FR, WIDTH), mean_state, land_mask, stations[None], observed[None], obs_weight[None]
     )
     updated, mean = place(result, increment, mean_forecast)
     return mean.reshape(mean_state.shape), updated.reshape(covariance.shape)

time: 103 us -> 94.4 us (0.917)
  local copies, waits for them, and re-layouts: 4.46 us -> 0 us
  Pallas kernels: 95.7 us -> 92 us
    pallas_call x1, Pallas kernels: 92.4 us -> 87.4 us  [filter_step(): pl.pallas_call(filter_kernel, out_shape=(jax.ShapeDtypeStruct((FR, NCOL,...]
    unnamed x6 -> x0, local copies, waits for them, and re-layouts: 2.92 us -> none
    reshape x3 -> x0, local copies, waits for them, and re-layouts: 1.54 us -> none  [the longest x1 0.83 us: local(): halves = mean_state.reshape(6, 2, HALO, width).transpose(1, 0, 2, 3)]
    pallas_call x1, Pallas kernels: 3.31 us -> 4.56 us  [place(): pl.pallas_call(place_kernel, grid=(NCOL // PAIR,), out_shape=(jax.ShapeDt...]
where the time goes in v4:
time: 94.4 us; the launch traced here: 92.6 us
  Pallas kernels  92 us (97%)
    pallas_call x1, Pallas kernels, filter_step(): pl.pallas_call(filter_kernel, out_shape=(jax.ShapeDtypeStruct((FR, NCOL,...  87.4 us
    pallas_call x1, Pallas kernels, place(): pl.pallas_call(place_kernel, grid=(NCOL // PAIR,), out_shape=(jax.ShapeDt...  4.56 us

profile of v4, /device:TPU:33, one launch (start us, length us, event | category | flops | bytes accessed | tf_op | source)
XLA Modules:
  0.0 92.6 jit_solution(6216037807181866786)
XLA Ops:
  0.6 87.4 %filter_step.1 = (bf16[96,16,256]{2,1,0:T(8,128)(2,1)}, f32[8,16,256]{2,1,0:T(8,128)}, f32[96,256]{1,0:T(8,128)}) custom-call(f32[16,96,256]{2,1,0:T(8,128)} %bitcast.6, f32[6,16,32]{2,1,0:T(8,128)} %mean_hbm.1, s32[512,256]{1,0:T(8,128)} %land_ref.1, s32[1,128]{1,0:T(1,128)} %bitcast.7, f32[1,128]{1,0:T(1,128)} %bitcast.8, f32[1,128]{1,0:T(1,128)} %bitcast.9), custom_call_target="tpu_custom_call" | custom-call | tf_op jit(solution)/shard_map/filter_step/pallas_call | solution.py:517
  88.0 4.6 %place.1 = (f32[16,96,256]{2,1,0:T(8,128)}, f32[96,32]{1,0:T(8,128)}) custom-call(bf16[96,16,256]{2,1,0:T(8,128)(2,1)} %get-tuple-element.7.result_ref, f32[8,16,256]{2,1,0:T(8,128)} %get-tuple-element.8.increment_ref, f32[96,256]{1,0:T(8,128)} %get-tuple-element.9.meanf_ref), custom_call_target="tpu_custom_call" | custom-call | tf_op jit(solution)/shard_map/place/pallas_call | solution.py:611

commit v5 on v4

--- a/solution.py
+++ b/solution.py
@@ -27,13 +27,6 @@
 
 def peer(c, s):
     return {"cols": c, "space": s}
-
-
-def greet(peers):
-    barrier = pltpu.get_barrier_semaphore()
-    for device in peers:
-        pl.semaphore_signal(barrier, inc=1, device_id=device, device_id_type=MESH)
-    pl.semaphore_wait(barrier, len(peers))
 
 
 def remote(src, dst, send, recv, device):
@@ -106,8 +99,8 @@
 
 
 CHUNKS = 8
-FIRST = 4
-ON0, FAR1, ON1 = 0, 1, 4
+FIRST = 8
+ON0, ON1 = 0, 1
 PER = NCOL // CHUNKS
 EDGE = PER * 6 * HALO
 GROUPS = 4
@@ -195,17 +188,17 @@
     last_run = jnp.where(zh == 0, y * 8 + 3, lax.rem(y + 3, 4) * 8 + 7)
 
     def start_halo(i):
-        odd = lax.rem(i, 2) == 1
-        slot = i // 4
-        inner = peer(c, run + 1 + lax.rem(i // 2, 2))
+        passed = i < 4
+        slot = jnp.minimum(i // 2, 1)
+        inner = peer(c, run + 1 + lax.rem(i, 2))
 
         def one(way, end, direct, source):
-            @pl.when(odd & end)
+            @pl.when(passed & end)
             def _():
                 at = relay.at[0, way, slot]
                 remote(source.at[i], at, halo_send.at[way, i], relay_recv.at[0, way, slot], inner).start()
 
-            @pl.when(jnp.logical_not(odd & end))
+            @pl.when(jnp.logical_not(passed & end))
             def _():
                 direct(i).start()
 
@@ -219,7 +212,7 @@
         )
 
     def relay_on(way, slot):
-        i = 4 * slot + 2 * x - 1
+        i = 2 * slot + x - 1
         goal = (above, below)[way].at[i]
         device = peer(c, (next_run, last_run)[way])
         return remote(relay.at[1, way, slot], goal, relay_send.at[1, way, slot], halo_recv.at[way, i], device)
@@ -278,6 +271,7 @@
         return carry
 
     lax.fori_loop(FIRST, CHUNKS, send_more, 0)
+    pass_far(1)
 
     lane = lax.broadcasted_iota(jnp.int32, (WIN, WIDTH), 1)
     first, last = lane == 0, lane == WIDTH - 1
@@ -328,10 +322,11 @@
         meanf_ref[pl.ds(TILE * f, TILE)] = fields[f][HALO : HALO + TILE]
     surface[pl.ds(NCOL * TILE, TILE)] = (fields[0] + fields[3])[HALO : HALO + TILE]
 
-    def advance(i, carry):
-        for at, action, slot in ((ON0, pass_on, 0), (FAR1, pass_far, 1), (ON1, pass_on, 1)):
-
-            @pl.when(i == at)
+    def advance(turn, carry):
+        i = lax.rem(turn + 4, CHUNKS)
+        for at, action, slot in ((ON0, pass_on, 0), (ON1, pass_on, 1)):
+
+            @pl.when(turn == at)
             def _():
                 action(slot)
 
@@ -522,7 +517,7 @@
             jax.ShapeDtypeStruct((FR, WIDTH), f32),
         ),
         in_specs=[HBM] * 6,
-        out_specs=(VMEM, VMEM, VMEM),
+        out_specs=(HBM, VMEM, VMEM),
         scratch_shapes=[
             pltpu.VMEM((NCOL, FR, WIDTH), f32),
             pltpu.VMEM((WIN, WIDTH), jnp.int32),
@@ -582,42 +577,58 @@
     )(cov, mean, land, stations, observed, weight)
 
 
-PAIR = 2
-
-
-def place_kernel(result_ref, increment_ref, meanf_ref, out_ref, mean_ref, held, total):
-    j = pl.program_id(0)
-
-    @pl.when(j == 0)
-    def _():
+PARTS = 4
+RUN = FR // PARTS
+
+
+def place_kernel(result_ref, increment_ref, meanf_ref, out_ref, mean_ref, low, held, made, total, in_sem, out_sem):
+    def load(q):
+        rows = pl.ds(q * RUN, RUN)
+        return pltpu.make_async_copy(result_ref.at[rows], low.at[rows], in_sem.at[q])
+
+    def store(q):
+        return pltpu.make_async_copy(made.at[q], out_ref.at[:, pl.ds(q * RUN, RUN)], out_sem.at[q])
+
+    for q in range(PARTS):
+        load(q).start()
+    for q in range(PARTS):
+        load(q).wait()
         for half in range(2):
-            part = result_ref[:, :, 128 * half : 128 * (half + 1)].astype(jnp.float32)
-            held[half] = part.reshape(FR * NCOL, 128)
-        for o in range(NC):
-            rows = pl.ds(o * PIECE, PIECE)
-            total[rows] = meanf_ref[rows] + increment_ref[o][:PIECE]
-        c = lax.axis_index("cols")
-        width = WIDTH // NC
-        turned = pltpu.roll(total[...], lax.rem(WIDTH - c * width, WIDTH), 1)
-        mean_ref[...] = turned[:, :width]
-
-    for n in range(PAIR):
-        for half in range(2):
-            out_ref[n, :, 128 * half : 128 * (half + 1)] = held[half, pl.ds(j * PAIR + n, FR, stride=NCOL)]
+            part = low[pl.ds(q * RUN, RUN), :, 128 * half : 128 * (half + 1)].astype(jnp.float32)
+            held[q % 2, half] = part.reshape(RUN * NCOL, 128)
+        for j in range(NCOL):
+            for half in range(2):
+                made[q, j, :, 128 * half : 128 * (half + 1)] = held[q % 2, half, pl.ds(j, RUN, stride=NCOL)]
+        store(q).start()
+    for o in range(NC):
+        rows = pl.ds(o * PIECE, PIECE)
+        total[rows] = meanf_ref[rows] + increment_ref[o][:PIECE]
+    c = lax.axis_index("cols")
+    width = WIDTH // NC
+    turned = pltpu.roll(total[...], lax.rem(WIDTH - c * width, WIDTH), 1)
+    mean_ref[...] = turned[:, :width]
+    for q in range(PARTS):
+        store(q).wait()
 
 
 def place(result, increment, mean_forecast):
-    whole = lambda shape: pl.BlockSpec(shape, lambda i: (0,) * len(shape))
+    dma = pltpu.SemaphoreType.DMA
     return pl.pallas_call(
         place_kernel,
-        grid=(NCOL // PAIR,),
         out_shape=(
             jax.ShapeDtypeStruct((NCOL, FR, WIDTH), jnp.float32),
             jax.ShapeDtypeStruct((FR, WIDTH // NC), jnp.float32),
         ),
-        in_specs=[whole((FR, NCOL, WIDTH)), whole((NC, NCOL, WIDTH)), whole((FR, WIDTH))],
-        out_specs=(pl.BlockSpec((PAIR, FR, WIDTH), lambda i: (i, 0, 0)), whole((FR, WIDTH // NC))),
-        scratch_shapes=[pltpu.VMEM((2, FR * NCOL, 128), jnp.float32), pltpu.VMEM((FR, WIDTH), jnp.float32)],
+        in_specs=[HBM, VMEM, VMEM],
+        out_specs=(HBM, VMEM),
+        scratch_shapes=[
+            pltpu.VMEM((FR, NCOL, WIDTH), jnp.bfloat16),
+            pltpu.VMEM((2, 2, RUN * NCOL, 128), jnp.float32),
+            pltpu.VMEM((PARTS, NCOL, RUN, WIDTH), jnp.float32),
+            pltpu.VMEM((FR, WIDTH), jnp.float32),
+            dma((PARTS,)),
+            dma((PARTS,)),
+        ],
         compiler_params=pltpu.CompilerParams(vmem_limit_bytes=60 * 1024 * 1024),
         name="place",
     )(result, increment, mean_forecast)

time: 94.4 us -> 91.7 us (0.971)
  Pallas kernels: 92 us -> 89.3 us
    pallas_call x1, Pallas kernels: 87.4 us -> 85.4 us  [filter_step(): pl.pallas_call(filter_kernel, out_shape=(jax.ShapeDtypeStruct((FR, NCOL,...]
where the time goes in v5:
time: 91.7 us; the launch traced here: 90 us
  Pallas kernels  89.3 us (97%)
    pallas_call x1, Pallas kernels, filter_step(): pl.pallas_call(filter_kernel, out_shape=(jax.ShapeDtypeStruct((FR, NCOL,...  85.4 us
    pallas_call x1, Pallas kernels, place(): pl.pallas_call(place_kernel, out_shape=(jax.ShapeDtypeStruct((NCOL, FR, W...  3.95 us

profile of v5, /device:TPU:33, one launch (start us, length us, event | category | flops | bytes accessed | tf_op | source)
XLA Modules:
  0.0 90.0 jit_solution(2027148917100345434)
XLA Ops:
  0.6 85.4 %filter_step.1 = (bf16[96,16,256]{2,1,0:T(8,128)(2,1)}, f32[8,16,256]{2,1,0:T(8,128)}, f32[96,256]{1,0:T(8,128)}) custom-call(f32[16,96,256]{2,1,0:T(8,128)} %bitcast.6, f32[6,16,32]{2,1,0:T(8,128)} %mean_hbm.1, s32[512,256]{1,0:T(8,128)} %land_ref.1, s32[1,128]{1,0:T(1,128)} %bitcast.7, f32[1,128]{1,0:T(1,128)} %bitcast.8, f32[1,128]{1,0:T(1,128)} %bitcast.9), custom_call_target="tpu_custom_call" | custom-call | tf_op jit(solution)/shard_map/filter_step/pallas_call | solution.py:512
  86.0 4.0 %place.1 = (f32[16,96,256]{2,1,0:T(8,128)}, f32[96,32]{1,0:T(8,128)}) custom-call(bf16[96,16,256]{2,1,0:T(8,128)(2,1)} %get-tuple-element.7.result_ref, f32[8,16,256]{2,1,0:T(8,128)} %get-tuple-element.8.increment_ref, f32[96,256]{1,0:T(8,128)} %get-tuple-element.9.meanf_ref), custom_call_target="tpu_custom_call" | custom-call | tf_op jit(solution)/shard_map/place/pallas_call | solution.py:616

commit v6 on v5

--- a/solution.py
+++ b/solution.py
@@ -100,7 +100,7 @@
 
 CHUNKS = 8
 FIRST = 8
-ON0, ON1 = 0, 1
+ON1 = 1
 PER = NCOL // CHUNKS
 EDGE = PER * 6 * HALO
 GROUPS = 4
@@ -290,6 +290,7 @@
     swap = remote(pieces.at[core], pieces.at[core], m_send.at[1, 0], m_recv.at[1, chip], peer(partner, s))
     swap.start()
     swap.wait()
+    pass_on(0)
     quarter = lax.broadcasted_iota(jnp.int32, (12, 128), 1) // 32
     for slot in range(4):
         for half in range(2):
@@ -324,7 +325,7 @@
 
     def advance(turn, carry):
         i = lax.rem(turn + 4, CHUNKS)
-        for at, action, slot in ((ON0, pass_on, 0), (ON1, pass_on, 1)):
+        for at, action, slot in ((ON1, pass_on, 1),):
 
             @pl.when(turn == at)
             def _():

time: 91.7 us -> 91.2 us (level)
  no operation moved by 1% of the time
where the time goes in v6:
time: 91.2 us; the launch traced here: 89.4 us
  Pallas kernels  88.8 us (97%)
    pallas_call x1, Pallas kernels, filter_step(): pl.pallas_call(filter_kernel, out_shape=(jax.ShapeDtypeStruct((FR, NCOL,...  84.8 us
    pallas_call x1, Pallas kernels, place(): pl.pallas_call(place_kernel, out_shape=(jax.ShapeDtypeStruct((NCOL, FR, W...  3.95 us

profile of v6, /device:TPU:33, one launch (start us, length us, event | category | flops | bytes accessed | tf_op | source)
XLA Modules:
  0.0 89.4 jit_solution(17275331862893525530)
XLA Ops:
  0.6 84.8 %filter_step.1 = (bf16[96,16,256]{2,1,0:T(8,128)(2,1)}, f32[8,16,256]{2,1,0:T(8,128)}, f32[96,256]{1,0:T(8,128)}) custom-call(f32[16,96,256]{2,1,0:T(8,128)} %bitcast.6, f32[6,16,32]{2,1,0:T(8,128)} %mean_hbm.1, s32[512,256]{1,0:T(8,128)} %land_ref.1, s32[1,128]{1,0:T(1,128)} %bitcast.7, f32[1,128]{1,0:T(1,128)} %bitcast.8, f32[1,128]{1,0:T(1,128)} %bitcast.9), custom_call_target="tpu_custom_call" | custom-call | tf_op jit(solution)/shard_map/filter_step/pallas_call | solution.py:513
  85.5 4.0 %place.1 = (f32[16,96,256]{2,1,0:T(8,128)}, f32[96,32]{1,0:T(8,128)}) custom-call(bf16[96,16,256]{2,1,0:T(8,128)(2,1)} %get-tuple-element.7.result_ref, f32[8,16,256]{2,1,0:T(8,128)} %get-tuple-element.8.increment_ref, f32[96,256]{1,0:T(8,128)} %get-tuple-element.9.meanf_ref), custom_call_target="tpu_custom_call" | custom-call | tf_op jit(solution)/shard_map/place/pallas_call | solution.py:617
